TPU v7x, 256 devices: a whole 4x4x8 slice. The times are simulated.
256 devices in a mesh: engine: 8 (over z_lo, core), ep: 32 (over y, z_hi, x).
Axes of the slice: x: 4, y: 4, z: 8 (z_hi: 2, z_lo: 4; z = z_hi * 4 + z_lo), core: 2. Of those that a mesh axis runs over, the one named last changes fastest.
Arguments:
- hidden_in: bfloat16 [65536, 7168], P(('engine', 'ep')), may hold values from -6 to 6
- expert_ids: int32 [65536, 8], P(('engine', 'ep')), may hold values from 0 to 255, all different within a row; in each aligned block of 256 rows (0 to 255, 256 to 511, ...) at most 16 rows name the same one
- route_weight: float32 [65536, 8], P(('engine', 'ep')), may hold values from 0.2 to 1
- gate_codes: bfloat16 [32, 7168, 256], P('ep', 'engine'), may hold values from -0.0625 to 0.0625
- gate_scales: bfloat16 [32, 56, 2], P('ep', 'engine'), may hold values from 0.29882812 to 3
- up_codes: bfloat16 [32, 7168, 256], P('ep', 'engine'), may hold values from -0.0625 to 0.0625
- up_scales: bfloat16 [32, 56, 2], P('ep', 'engine'), may hold values from 0.29882812 to 3
- down_codes: bfloat16 [32, 256, 7168], P('ep', None, 'engine'), may hold values from -0.125 to 0.125
- down_scales: bfloat16 [32, 2, 56], P('ep', None, 'engine'), may hold values from 0.29882812 to 3
- bucket_owner: int32 [32, 8], P('ep'), may hold values from 0 to 7, each once within a row
Outputs:
- mixed: bfloat16 [65536, 7168], P(('engine', 'ep'))
Inputs may be any that keep to these rules, and one draw needn't show every extreme that they name: `expert_ids`: the 8 ids of one token differ; among the 256 tokens of one device no expert is named more than 16 times. `bucket_owner`: each row holds each engine index once.
All inputs are finite; a program needn't handle non-finite values.
Results may differ from a plain program's by a relative error of at most 0.0081.
Values may be sent and summed in bfloat16 or wider, within the bound.
A program may use at most 128 MiB of HBM per device.

v0:
```python
import jax
import jax.numpy as jnp
from jax import lax
from jax.sharding import PartitionSpec as P

D = 7168
SPLIT = 8
BLOCK = 128
CAP = 16


def from_behind(value, axis, steps):
    count = lax.axis_size(axis)
    pairs = [(source, (source + steps) % count) for source in range(count)]
    return lax.ppermute(value, axis, pairs)


def dequantize(values, scale_blocks):
    row_count, col_count = values.shape
    blocks = values.astype(jnp.float32).reshape(
        row_count // BLOCK, BLOCK, col_count // BLOCK, BLOCK
    )
    scaled = blocks * scale_blocks.astype(jnp.float32)[:, None, :, None]
    return scaled.reshape(row_count, col_count).astype(jnp.bfloat16)


def pick_rows(pieces, picks):
    stacked = jnp.stack(pieces, axis=0)
    chosen = jnp.take(stacked, picks, axis=0)
    return chosen.reshape((chosen.shape[0] * chosen.shape[1],) + chosen.shape[2:])


def pick_columns(pieces, picks):
    stacked = jnp.stack(pieces, axis=0)
    chosen = jnp.take(stacked, picks, axis=0)
    return chosen.transpose(1, 0, 2).reshape(chosen.shape[1], chosen.shape[0] * chosen.shape[2])


def routing_tables(choices, weights, experts, capacity):
    labels = jnp.arange(experts, dtype=jnp.int32)
    matches = (choices[:, :, None] == labels[None, None, :]).astype(jnp.int32)
    per_token = jnp.sum(matches, axis=1)
    before = jnp.cumsum(per_token, axis=0) - per_token
    slot_index = jnp.sum(matches * before[:, None, :], axis=2)
    is_live = jnp.sum(matches, axis=2)
    target = jnp.where(is_live > 0, choices * capacity + slot_index, -1)
    places = jnp.arange(experts * capacity, dtype=jnp.int32)
    matched = target[:, :, None] == places[None, None, :]
    placing = jnp.sum(matched.astype(jnp.float32), axis=1)
    combining = jnp.sum(jnp.where(matched, weights[:, :, None], jnp.float32(0.0)), axis=1)
    return (placing, combining)


def on_device(
    hidden_in,
    expert_ids,
    route_weight,
    gate_codes,
    gate_scales,
    up_codes,
    up_scales,
    down_codes,
    down_scales,
    bucket_owner,
):
    ep_count = lax.axis_size("ep")
    experts = ep_count // SPLIT
    owners = bucket_owner[0]
    own_shard = (
        gate_codes[0],
        up_codes[0],
        down_codes[0],
        gate_scales[0],
        up_scales[0],
        down_scales[0],
    )
    engine_count = lax.axis_size("engine")
    arrived = [own_shard]
    for offset in range(1, engine_count):
        arrived.append(
            from_behind(
                (
                    own_shard[0],
                    own_shard[1],
                    own_shard[2],
                    own_shard[3],
                    own_shard[4],
                    own_shard[5],
                ),
                "engine",
                offset,
            )
        )
    picks = jnp.mod(lax.axis_index("engine") - owners, engine_count)
    gate_full = pick_rows([parcel[0] for parcel in arrived], picks)
    up_full = pick_rows([parcel[1] for parcel in arrived], picks)
    down_full = pick_columns([parcel[2] for parcel in arrived], picks)
    gate_scale = pick_rows([parcel[3] for parcel in arrived], picks)
    up_scale = pick_rows([parcel[4] for parcel in arrived], picks)
    down_scale = pick_columns([parcel[5] for parcel in arrived], picks)
    gate_w = dequantize(gate_full, gate_scale)
    up_w = dequantize(up_full, up_scale)
    down_w = dequantize(down_full, down_scale)
    placing, combining = routing_tables(expert_ids, route_weight, experts, CAP)
    send_rows = jnp.dot(
        placing.T.astype(jnp.bfloat16), hidden_in, preferred_element_type=jnp.float32
    ).astype(jnp.bfloat16)
    outgoing = jnp.broadcast_to(
        send_rows.reshape(experts, 1, CAP, D), (experts, SPLIT, CAP, D)
    ).reshape(ep_count, CAP, D)
    arrived_rows = lax.all_to_all(outgoing, "ep", split_axis=0, concat_axis=0, tiled=True)
    expert_rows = arrived_rows.reshape(ep_count * CAP, D)
    gate_act = jnp.dot(expert_rows, gate_w, preferred_element_type=jnp.float32)
    up_act = jnp.dot(expert_rows, up_w, preferred_element_type=jnp.float32)
    hidden = (jax.nn.silu(gate_act) * up_act).astype(jnp.bfloat16)
    partial_out = (
        jnp.dot(hidden, down_w, preferred_element_type=jnp.float32)
        .astype(jnp.bfloat16)
        .reshape(ep_count, CAP, D)
    )
    returned = lax.all_to_all(partial_out, "ep", split_axis=0, concat_axis=0, tiled=True)
    expert_sums = (
        jnp.sum(returned.astype(jnp.float32).reshape(experts, SPLIT, CAP, D), axis=1)
        .reshape(experts * CAP, D)
        .astype(jnp.bfloat16)
    )
    mixed = jnp.dot(combining, expert_sums.astype(jnp.float32), precision=lax.Precision.HIGHEST)
    return mixed.astype(jnp.bfloat16)


def solution(mesh):
    in_specs = (
        P(("engine", "ep"), None),
        P(("engine", "ep"), None),
        P(("engine", "ep"), None),
        P("ep", "engine", None),
        P("ep", "engine", None),
        P("ep", "engine", None),
        P("ep", "engine", None),
        P("ep", None, "engine"),
        P("ep", None, "engine"),
        P("ep", None),
    )
    out_specs = P(("engine", "ep"), None)
    return jax.shard_map(
        on_device, mesh=mesh, in_specs=in_specs, out_specs=out_specs, check_vma=False
    )
```

profile of v0, /device:TPU:2, one launch (start us, length us, event | category | flops | bytes accessed | tf_op | source)
XLA Modules:
  0.0 739.1 jit_solution(8421206427764232009)
XLA Ops:
  17.0 13.5 %all-to-all-start = ((bf16[32,16,7168]{2,1,0:T(8,128)(2,1)}), bf16[32,16,7168]{2,1,0:T(8,128)(2,1)}, u32[]{:S(2)}, u32[]{:S(2)}) async-start(bf16[32,16,7168]{2,1,0:T(8,128)(2,1)} %bitcast.157), calls=%async_computation | async-start | bytes 14680064 | tf_op jit(solution)/shard_map/all_to_all | solution.py:111
  33.1 31.3 %collective-permute-done.7 = bf16[7,2]{0,1:T(2,128)(2,1)S(1)} collective-permute-done((bf16[7,2]{0,1:T(2,128)(2,1)}, bf16[7,2]{0,1:T(2,128)(2,1)S(1)}, u32[]{:S(2)}, u32[]{:S(2)}) %collective-permute-start.7) | collective-permute-done | bytes 60 | tf_op jit(solution)/shard_map/ppermute | solution.py:15
  64.4 24.5 %collective-permute-start.8 = (bf16[7,2]{0,1:T(2,128)(2,1)S(1)}, bf16[7,2]{0,1:T(2,128)(2,1)S(1)}, u32[]{:S(2)}, u32[]{:S(2)}) collective-permute-start(bf16[7,2]{0,1:T(2,128)(2,1)S(1)} %bitcast.188), channel_id=1, source_target_pairs={{0,64},{32,96},{64,128},{96,160},{128,192},{160,224},{192,0},{224,... | collective-permute-start | bytes 92 | tf_op jit(solution)/shard_map/ppermute | solution.py:15
  88.9 105.5 %collective-permute-done.8 = bf16[7,2]{0,1:T(2,128)(2,1)S(1)} collective-permute-done((bf16[7,2]{0,1:T(2,128)(2,1)S(1)}, bf16[7,2]{0,1:T(2,128)(2,1)S(1)}, u32[]{:S(2)}, u32[]{:S(2)}) %collective-permute-start.8) | collective-permute-done | bytes 60 | tf_op jit(solution)/shard_map/ppermute | solution.py:15
  194.4 18.8 %collective-permute-start.9 = (bf16[7,2]{0,1:T(2,128)(2,1)S(1)}, bf16[7,2]{0,1:T(2,128)(2,1)S(1)}, u32[]{:S(2)}, u32[]{:S(2)}) collective-permute-start(bf16[7,2]{0,1:T(2,128)(2,1)S(1)} %bitcast.189), channel_id=1, source_target_pairs={{0,96},{32,128},{64,160},{96,192},{128,224},{160,0},{192,32},{224,... | collective-permute-start | bytes 92 | tf_op jit(solution)/shard_map/ppermute | solution.py:15
  214.6 5.7 collective-permute-start.10
  301.5 7.7 %collective-permute-done.5 = bf16[896,256]{1,0:T(8,128)(2,1)S(1)} collective-permute-done((bf16[896,256]{1,0:T(8,128)(2,1)S(1)}, bf16[896,256]{1,0:T(8,128)(2,1)S(1)}, u32[]{:S(2)}, u32[]{:S(2)}) %collective-permute-start.5) | collective-permute-done | bytes 458784 | tf_op jit(solution)/shard_map/ppermute | solution.py:15
  309.2 19.4 %collective-permute-start.17 = (bf16[896,256]{1,0:T(8,128)(2,1)S(1)}, bf16[896,256]{1,0:T(8,128)(2,1)S(1)}, u32[]{:S(2)}, u32[]{:S(2)}) collective-permute-start(bf16[896,256]{1,0:T(8,128)(2,1)S(1)} %bitcast.174), channel_id=1, source_target_pairs={{0,128},{32,160},{64,192},{96,224},{128,0},{160,32},{192,64},{224,... | collective-permute-start | bytes 1376264 | tf_op jit(solution)/shard_map/ppermute | solution.py:15
  334.9 29.8 %collective-permute-start.19 = (bf16[896,256]{1,0:T(8,128)(2,1)S(1)}, bf16[896,256]{1,0:T(8,128)(2,1)S(1)}, u32[]{:S(2)}, u32[]{:S(2)}) collective-permute-start(bf16[896,256]{1,0:T(8,128)(2,1)S(1)} %bitcast.176), channel_id=1, source_target_pairs={{0,192},{32,224},{64,0},{96,32},{128,64},{160,96},{192,128},{224,1... | collective-permute-start | bytes 1376264 | tf_op jit(solution)/shard_map/ppermute | solution.py:15
  371.7 21.0 %collective-permute-start.29 = (bf16[256,896]{1,0:T(8,128)(2,1)S(1)}, bf16[256,896]{1,0:T(8,128)(2,1)S(1)}, u32[]{:S(2)}, u32[]{:S(2)}) collective-permute-start(bf16[256,896]{1,0:T(8,128)(2,1)S(1)} %bitcast.179), channel_id=1, source_target_pairs={{0,64},{32,96},{64,128},{96,160},{128,192},{160,224},{192,0},{224,... | collective-permute-start | bytes 1376264 | tf_op jit(solution)/shard_map/ppermute | solution.py:15
  396.0 11.3 %collective-permute-start.31 = (bf16[256,896]{1,0:T(8,128)(2,1)S(1)}, bf16[256,896]{1,0:T(8,128)(2,1)S(1)}, u32[]{:S(2)}, u32[]{:S(2)}) collective-permute-start(bf16[256,896]{1,0:T(8,128)(2,1)S(1)} %bitcast.181), channel_id=1, source_target_pairs={{0,128},{32,160},{64,192},{96,224},{128,0},{160,32},{192,64},{224,... | collective-permute-start | bytes 1376264 | tf_op jit(solution)/shard_map/ppermute | solution.py:15
  408.0 14.3 %collective-permute-start.32 = (bf16[256,896]{1,0:T(8,128)(2,1)S(1)}, bf16[256,896]{1,0:T(8,128)(2,1)S(1)}, u32[]{:S(2)}, u32[]{:S(2)}) collective-permute-start(bf16[256,896]{1,0:T(8,128)(2,1)S(1)} %bitcast.182), channel_id=1, source_target_pairs={{0,160},{32,192},{64,224},{96,0},{128,32},{160,64},{192,96},{224,1... | collective-permute-start | bytes 1376264 | tf_op jit(solution)/shard_map/ppermute | solution.py:15
  427.8 9.3 %select_convert_fusion.1 = (f32[8,896,256]{2,1,0:T(8,128)}, f32[8,896,256]{2,1,0:T(8,128)}) fusion(bf16[8,896,256]{2,1,0:T(8,128)(2,1)} %gather_fusion.2, pred[8]{0:T(512)(128)(4,1)S(1)} %get-tuple-element.11, bf16[8,896,256]{2,1,0:T(8,128)(2,1)} %gather_fusion.4), kind=kLoop, calls=%fused_computation.22 | loop fusion | flops 7340032 | bytes 22020104 | tf_op jit(solution)/shard_map/convert_element_type | solution.py:20
  437.1 10.3 %reshape.188 = f32[56,128,2,128]{3,2,1,0:T(2,128)} reshape(f32[8,896,256]{2,1,0:T(8,128)} %get-tuple-element.15) | data formatting | bytes 14680064 | tf_op jit(solution)/shard_map/convert_element_type | solution.py:20
  447.4 10.3 %reshape.190 = f32[56,128,2,128]{3,2,1,0:T(2,128)} reshape(f32[8,896,256]{2,1,0:T(8,128)} %get-tuple-element.16) | data formatting | bytes 14680064 | tf_op jit(solution)/shard_map/convert_element_type | solution.py:20
  457.6 15.6 %collective-permute-start.33 = (bf16[256,896]{1,0:T(8,128)(2,1)S(1)}, bf16[256,896]{1,0:T(8,128)(2,1)S(1)}, u32[]{:S(2)}, u32[]{:S(2)}) collective-permute-start(bf16[256,896]{1,0:T(8,128)(2,1)S(1)} %bitcast.183), channel_id=1, source_target_pairs={{0,192},{32,224},{64,0},{96,32},{128,64},{160,96},{192,128},{224,1... | collective-permute-start | bytes 1376264 | tf_op jit(solution)/shard_map/ppermute | solution.py:15
  492.5 5.5 convert_bitcast_fusion
  498.0 8.5 %copy.73 = f32[256,8,896]{0,2,1:T(8,128)} copy(f32[256,8,896]{2,0,1:T(8,128)} %convert_bitcast_fusion) | data formatting | bytes 14680064 | tf_op jit(solution)/shard_map/convert_element_type | solution.py:20
  506.5 8.7 %multiply_convert_fusion.1 = bf16[56,128,2,128]{3,2,1,0:T(2,128)(2,1)} fusion(f32[56,128,2,128]{3,2,1,0:T(2,128)} %reshape.188, f32[56,2]{1,0:T(8,128)S(1)} %copy.69), kind=kLoop, calls=%fused_computation.14 | loop fusion | flops 3670016 | bytes 11010496 | tf_op jit(solution)/shard_map/convert_element_type | solution.py:24
  515.1 8.7 %multiply_convert_fusion = bf16[56,128,2,128]{3,2,1,0:T(2,128)(2,1)} fusion(f32[56,128,2,128]{3,2,1,0:T(2,128)} %reshape.190, f32[56,2]{1,0:T(8,128)S(1)} %copy.72), kind=kLoop, calls=%fused_computation.13 | loop fusion | flops 3670016 | bytes 11010496 | tf_op jit(solution)/shard_map/convert_element_type | solution.py:24
  528.7 5.7 fusion
  534.5 6.2 fusion.4
  540.7 16.0 %convolution_convert_fusion = bf16[512,7168]{1,0:T(8,128)(2,1)} fusion(bf16[256,7168]{0,1:T(8,128)(2,1)} %fusion, bf16[512,7168]{1,0:T(8,128)(2,1)} %bitcast.5, bf16[896,8,2,128]{3,2,1,0:T(2,128)(2,1)} %bitcast.161, f32[512,256]{1,0:T(8,128)S(1)} %fusion.4), kind=kOutput, calls=%fused_computation.6 | convolution fusion | flops 3762552832 | bytes 22544384 | tf_op jit(solution)/shard_map/dot_general | solution.py:117
  556.6 176.5 %all_to_all.10 = bf16[32,16,7168]{2,1,0:T(8,128)(2,1)S(1)} all-to-all(bf16[32,16,7168]{2,1,0:T(8,128)(2,1)} %bitcast.159), channel_id=1, replica_groups=mesh['engine'=8,'ep'=32] {'ep'}, dimensions={0} | all-to-all | bytes 14680064 | tf_op jit(solution)/shard_map/all_to_all | solution.py:121
  (178 shorter events, 154.7 us)
Async XLA Ops:
  0.0 289.2 %collective-permute-start = (bf16[896,256]{1,0:T(8,128)(2,1)}, bf16[896,256]{1,0:T(8,128)(2,1)S(1)}, u32[]{:S(2)}, u32[]{:S(2)}) collective-permute-start(bf16[896,256]{1,0:T(8,128)(2,1)} %bitcast.164), channel_id=1, source_target_pairs={{0,32},{32,64},{64,96},{96,128},{128,160},{160,192},{192,224},{224... | collective-permute-start | bytes 1376264 | tf_op jit(solution)/shard_map/ppermute | solution.py:15
  0.0 290.1 %collective-permute-start.1 = (bf16[896,256]{1,0:T(8,128)(2,1)}, bf16[896,256]{1,0:T(8,128)(2,1)S(1)}, u32[]{:S(2)}, u32[]{:S(2)}) collective-permute-start(bf16[896,256]{1,0:T(8,128)(2,1)} %bitcast.165), channel_id=1, source_target_pairs={{0,64},{32,96},{64,128},{96,160},{128,192},{160,224},{192,0},{224,... | collective-permute-start | bytes 1376264 | tf_op jit(solution)/shard_map/ppermute | solution.py:15
  2.0 290.2 %collective-permute-start.2 = (bf16[896,256]{1,0:T(8,128)(2,1)}, bf16[896,256]{1,0:T(8,128)(2,1)S(1)}, u32[]{:S(2)}, u32[]{:S(2)}) collective-permute-start(bf16[896,256]{1,0:T(8,128)(2,1)} %bitcast.166), channel_id=1, source_target_pairs={{0,96},{32,128},{64,160},{96,192},{128,224},{160,0},{192,32},{224,... | collective-permute-start | bytes 1376264 | tf_op jit(solution)/shard_map/ppermute | solution.py:15
  5.2 287.7 %collective-permute-start.3 = (bf16[896,256]{1,0:T(8,128)(2,1)}, bf16[896,256]{1,0:T(8,128)(2,1)S(1)}, u32[]{:S(2)}, u32[]{:S(2)}) collective-permute-start(bf16[896,256]{1,0:T(8,128)(2,1)} %bitcast.167), channel_id=1, source_target_pairs={{0,128},{32,160},{64,192},{96,224},{128,0},{160,32},{192,64},{224,... | collective-permute-start | bytes 1376264 | tf_op jit(solution)/shard_map/ppermute | solution.py:15
  5.7 58.7 %collective-permute-start.7 = (bf16[7,2]{0,1:T(2,128)(2,1)}, bf16[7,2]{0,1:T(2,128)(2,1)S(1)}, u32[]{:S(2)}, u32[]{:S(2)}) collective-permute-start(bf16[7,2]{0,1:T(2,128)(2,1)} %bitcast.187), channel_id=1, source_target_pairs={{0,32},{32,64},{64,96},{96,128},{128,160},{160,192},{192,224},{224... | collective-permute-start | bytes 92 | tf_op jit(solution)/shard_map/ppermute | solution.py:15
  17.0 517.4 %all-to-all-start = ((bf16[32,16,7168]{2,1,0:T(8,128)(2,1)}), bf16[32,16,7168]{2,1,0:T(8,128)(2,1)}, u32[]{:S(2)}, u32[]{:S(2)}) async-start(bf16[32,16,7168]{2,1,0:T(8,128)(2,1)} %bitcast.157), calls=%async_computation | async-start | bytes 14680064 | tf_op jit(solution)/shard_map/all_to_all | solution.py:111
  64.4 130.0 %collective-permute-start.8 = (bf16[7,2]{0,1:T(2,128)(2,1)S(1)}, bf16[7,2]{0,1:T(2,128)(2,1)S(1)}, u32[]{:S(2)}, u32[]{:S(2)}) collective-permute-start(bf16[7,2]{0,1:T(2,128)(2,1)S(1)} %bitcast.188), channel_id=1, source_target_pairs={{0,64},{32,96},{64,128},{96,160},{128,192},{160,224},{192,0},{224,... | collective-permute-start | bytes 92 | tf_op jit(solution)/shard_map/ppermute | solution.py:15
  194.4 20.2 %collective-permute-start.9 = (bf16[7,2]{0,1:T(2,128)(2,1)S(1)}, bf16[7,2]{0,1:T(2,128)(2,1)S(1)}, u32[]{:S(2)}, u32[]{:S(2)}) collective-permute-start(bf16[7,2]{0,1:T(2,128)(2,1)S(1)} %bitcast.189), channel_id=1, source_target_pairs={{0,96},{32,128},{64,160},{96,192},{128,224},{160,0},{192,32},{224,... | collective-permute-start | bytes 92 | tf_op jit(solution)/shard_map/ppermute | solution.py:15
  284.7 14.6 %collective-permute-start.4 = (bf16[896,256]{1,0:T(8,128)(2,1)S(1)}, bf16[896,256]{1,0:T(8,128)(2,1)}, u32[]{:S(2)}, u32[]{:S(2)}) collective-permute-start(bf16[896,256]{1,0:T(8,128)(2,1)S(1)} %bitcast.168), channel_id=1, source_target_pairs={{0,160},{32,192},{64,224},{96,0},{128,32},{160,64},{192,96},{224,1... | collective-permute-start | bytes 1376264 | tf_op jit(solution)/shard_map/ppermute | solution.py:15
  289.2 19.9 %collective-permute-start.5 = (bf16[896,256]{1,0:T(8,128)(2,1)S(1)}, bf16[896,256]{1,0:T(8,128)(2,1)S(1)}, u32[]{:S(2)}, u32[]{:S(2)}) collective-permute-start(bf16[896,256]{1,0:T(8,128)(2,1)S(1)} %bitcast.169), channel_id=1, source_target_pairs={{0,192},{32,224},{64,0},{96,32},{128,64},{160,96},{192,128},{224,1... | collective-permute-start | bytes 1376264 | tf_op jit(solution)/shard_map/ppermute | solution.py:15
  290.1 39.2 %collective-permute-start.6 = (bf16[896,256]{1,0:T(8,128)(2,1)S(1)}, bf16[896,256]{1,0:T(8,128)(2,1)S(1)}, u32[]{:S(2)}, u32[]{:S(2)}) collective-permute-start(bf16[896,256]{1,0:T(8,128)(2,1)S(1)} %bitcast.170), channel_id=1, source_target_pairs={{0,224},{32,0},{64,32},{96,64},{128,96},{160,128},{192,160},{224,1... | collective-permute-start | bytes 1376264 | tf_op jit(solution)/shard_map/ppermute | solution.py:15
  292.1 42.8 %collective-permute-start.14 = (bf16[896,256]{1,0:T(8,128)(2,1)S(1)}, bf16[896,256]{1,0:T(8,128)(2,1)S(1)}, u32[]{:S(2)}, u32[]{:S(2)}) collective-permute-start(bf16[896,256]{1,0:T(8,128)(2,1)S(1)} %bitcast.171), channel_id=1, source_target_pairs={{0,32},{32,64},{64,96},{96,128},{128,160},{160,192},{192,224},{224... | collective-permute-start | bytes 1376264 | tf_op jit(solution)/shard_map/ppermute | solution.py:15
  292.9 72.6 %collective-permute-start.15 = (bf16[896,256]{1,0:T(8,128)(2,1)S(1)}, bf16[896,256]{1,0:T(8,128)(2,1)S(1)}, u32[]{:S(2)}, u32[]{:S(2)}) collective-permute-start(bf16[896,256]{1,0:T(8,128)(2,1)S(1)} %bitcast.172), channel_id=1, source_target_pairs={{0,64},{32,96},{64,128},{96,160},{128,192},{160,224},{192,0},{224,... | collective-permute-start | bytes 1376264 | tf_op jit(solution)/shard_map/ppermute | solution.py:15
  299.3 67.0 %collective-permute-start.16 = (bf16[896,256]{1,0:T(8,128)(2,1)S(1)}, bf16[896,256]{1,0:T(8,128)(2,1)S(1)}, u32[]{:S(2)}, u32[]{:S(2)}) collective-permute-start(bf16[896,256]{1,0:T(8,128)(2,1)S(1)} %bitcast.173), channel_id=1, source_target_pairs={{0,96},{32,128},{64,160},{96,192},{128,224},{160,0},{192,32},{224,... | collective-permute-start | bytes 1376264 | tf_op jit(solution)/shard_map/ppermute | solution.py:15
  309.2 62.5 %collective-permute-start.17 = (bf16[896,256]{1,0:T(8,128)(2,1)S(1)}, bf16[896,256]{1,0:T(8,128)(2,1)S(1)}, u32[]{:S(2)}, u32[]{:S(2)}) collective-permute-start(bf16[896,256]{1,0:T(8,128)(2,1)S(1)} %bitcast.174), channel_id=1, source_target_pairs={{0,128},{32,160},{64,192},{96,224},{128,0},{160,32},{192,64},{224,... | collective-permute-start | bytes 1376264 | tf_op jit(solution)/shard_map/ppermute | solution.py:15
  329.4 64.1 %collective-permute-start.18 = (bf16[896,256]{1,0:T(8,128)(2,1)S(1)}, bf16[896,256]{1,0:T(8,128)(2,1)}, u32[]{:S(2)}, u32[]{:S(2)}) collective-permute-start(bf16[896,256]{1,0:T(8,128)(2,1)S(1)} %bitcast.175), channel_id=1, source_target_pairs={{0,160},{32,192},{64,224},{96,0},{128,32},{160,64},{192,96},{224,1... | collective-permute-start | bytes 1376264 | tf_op jit(solution)/shard_map/ppermute | solution.py:15
  334.9 61.1 %collective-permute-start.19 = (bf16[896,256]{1,0:T(8,128)(2,1)S(1)}, bf16[896,256]{1,0:T(8,128)(2,1)S(1)}, u32[]{:S(2)}, u32[]{:S(2)}) collective-permute-start(bf16[896,256]{1,0:T(8,128)(2,1)S(1)} %bitcast.176), channel_id=1, source_target_pairs={{0,192},{32,224},{64,0},{96,32},{128,64},{160,96},{192,128},{224,1... | collective-permute-start | bytes 1376264 | tf_op jit(solution)/shard_map/ppermute | solution.py:15
  365.5 42.5 %collective-permute-start.20 = (bf16[896,256]{1,0:T(8,128)(2,1)S(1)}, bf16[896,256]{1,0:T(8,128)(2,1)S(1)}, u32[]{:S(2)}, u32[]{:S(2)}) collective-permute-start(bf16[896,256]{1,0:T(8,128)(2,1)S(1)} %bitcast.177), channel_id=1, source_target_pairs={{0,224},{32,0},{64,32},{96,64},{128,96},{160,128},{192,160},{224,1... | collective-permute-start | bytes 1376264 | tf_op jit(solution)/shard_map/ppermute | solution.py:15
  366.3 91.3 %collective-permute-start.28 = (bf16[256,896]{1,0:T(8,128)(2,1)S(1)}, bf16[256,896]{1,0:T(8,128)(2,1)S(1)}, u32[]{:S(2)}, u32[]{:S(2)}) collective-permute-start(bf16[256,896]{1,0:T(8,128)(2,1)S(1)} %bitcast.178), channel_id=1, source_target_pairs={{0,32},{32,64},{64,96},{96,128},{128,160},{160,192},{192,224},{224... | collective-permute-start | bytes 1376264 | tf_op jit(solution)/shard_map/ppermute | solution.py:15
  371.7 102.4 %collective-permute-start.29 = (bf16[256,896]{1,0:T(8,128)(2,1)S(1)}, bf16[256,896]{1,0:T(8,128)(2,1)S(1)}, u32[]{:S(2)}, u32[]{:S(2)}) collective-permute-start(bf16[256,896]{1,0:T(8,128)(2,1)S(1)} %bitcast.179), channel_id=1, source_target_pairs={{0,64},{32,96},{64,128},{96,160},{128,192},{160,224},{192,0},{224,... | collective-permute-start | bytes 1376264 | tf_op jit(solution)/shard_map/ppermute | solution.py:15
  393.5 81.8 %collective-permute-start.30 = (bf16[256,896]{1,0:T(8,128)(2,1)S(1)}, bf16[256,896]{1,0:T(8,128)(2,1)S(1)}, u32[]{:S(2)}, u32[]{:S(2)}) collective-permute-start(bf16[256,896]{1,0:T(8,128)(2,1)S(1)} %bitcast.180), channel_id=1, source_target_pairs={{0,96},{32,128},{64,160},{96,192},{128,224},{160,0},{192,32},{224,... | collective-permute-start | bytes 1376264 | tf_op jit(solution)/shard_map/ppermute | solution.py:15
  396.0 80.1 %collective-permute-start.31 = (bf16[256,896]{1,0:T(8,128)(2,1)S(1)}, bf16[256,896]{1,0:T(8,128)(2,1)S(1)}, u32[]{:S(2)}, u32[]{:S(2)}) collective-permute-start(bf16[256,896]{1,0:T(8,128)(2,1)S(1)} %bitcast.181), channel_id=1, source_target_pairs={{0,128},{32,160},{64,192},{96,224},{128,0},{160,32},{192,64},{224,... | collective-permute-start | bytes 1376264 | tf_op jit(solution)/shard_map/ppermute | solution.py:15
  408.0 68.8 %collective-permute-start.32 = (bf16[256,896]{1,0:T(8,128)(2,1)S(1)}, bf16[256,896]{1,0:T(8,128)(2,1)S(1)}, u32[]{:S(2)}, u32[]{:S(2)}) collective-permute-start(bf16[256,896]{1,0:T(8,128)(2,1)S(1)} %bitcast.182), channel_id=1, source_target_pairs={{0,160},{32,192},{64,224},{96,0},{128,32},{160,64},{192,96},{224,1... | collective-permute-start | bytes 1376264 | tf_op jit(solution)/shard_map/ppermute | solution.py:15
  457.6 24.3 %collective-permute-start.33 = (bf16[256,896]{1,0:T(8,128)(2,1)S(1)}, bf16[256,896]{1,0:T(8,128)(2,1)S(1)}, u32[]{:S(2)}, u32[]{:S(2)}) collective-permute-start(bf16[256,896]{1,0:T(8,128)(2,1)S(1)} %bitcast.183), channel_id=1, source_target_pairs={{0,192},{32,224},{64,0},{96,32},{128,64},{160,96},{192,128},{224,1... | collective-permute-start | bytes 1376264 | tf_op jit(solution)/shard_map/ppermute | solution.py:15
  (27 other events, 191.2 us)
where the time goes:
time: 749 us; the launch traced here: 739 us
  waiting for transfers between devices  216 us (29%)
  starting transfers between devices  196 us (26%)
  blocking collectives  177 us (24%)
  local copies, waits for them, and re-layouts  76.4 us (10%)
  other arithmetic  43.6 us (6%)
  matrix products  29.5 us (4%)
    ppermute x42, waiting for transfers between devices, from_behind(): return lax.ppermute(value, axis, pairs)  216 us
    ppermute x42, starting transfers between devices, from_behind(): return lax.ppermute(value, axis, pairs)  183 us
    all_to_all x1, blocking collectives, on_device(): lax.all_to_all(partial_out, 'ep', split_axis=0, concat_axis=0, tiled=True)  177 us
    convert_element_type x3, local copies, waits for them, and re-layouts, dequantize(): values.astype(jnp.float32)  29 us
    convert_element_type x3, other arithmetic, dequantize(): return scaled.reshape(row_count, col_count).astype(jnp.bfloat16)  23.1 us
    unnamed x58, local copies, waits for them, and re-layouts  19.1 us
    dot_general x1, matrix products, on_device(): jnp.dot(hidden, down_w, preferred_element_type=jnp.float32)  16 us
  transfers between devices with their start and end apart: 43, of which 26 were waited for; matrix products, arithmetic and copies ran while one was open for 16% of the time, Pallas kernels for 0%

commit v1 on v0

v1 whole, which is shorter than its diff:
```python
import functools

import jax
import jax.numpy as jnp
from jax import lax
from jax.experimental import pallas as pl
from jax.experimental.pallas import tpu as pltpu
from jax.sharding import PartitionSpec as P

D = 7168
BLOCK = 128
CAP = 16
NB = 8
BUCKET = D // NB
HID = 256
TOK = 256
LIVE = 4
SLOTS = LIVE * CAP
PLANE = 16
ROWS = PLANE * CAP
SUBS = (256, 256, 256, 128)
OFFS = (0, 256, 512, 768)
NJ = len(SUBS)
MESH = pl.DeviceIdType.MESH


def kernel(
    hid_hbm, ids_ref, rw_ref, gc_hbm, uc_hbm, dc_hbm, gs_ref, us_ref, ds_ref, own_ref,
    es_ref, comb_ref,
    G, U, Ds, X, S, hid_v, acc, H, Ps, Rs, row_tx, row_rx, row_sm, inv_sm, tab_sm,
    load_sem, hid_sem, ring_s, ring_r, dring_s, dring_r, sib_s, sib_r, dsib_s, dsib_r,
    disp_s, disp_r, ret_s, ret_r, row_s, row_r, row_l,
):
    eng = lax.axis_index("engine")
    ep = lax.axis_index("ep")
    z_lo, core = eng // 2, eng % 2
    x, z_hi, y = ep % 4, (ep // 4) % 2, ep // 8
    z = z_hi * 4 + z_lo
    me_xy = y * 4 + x

    def dev(xx, yy, zz, cc):
        return ((zz % 4) * 2 + cc, (yy * 2 + zz // 4) * 4 + xx)

    ring_dev = (dev(x, y, (z + 1) % 8, core), dev(x, y, (z + 7) % 8, core))
    sib_dev = dev(x, y, z, 1 - core)
    far_dev = dev(x, y, (z + 4) % 8, core)

    def plane_dev(d):
        xx, yy = (x + d % 4) % 4, (y + d // 4) % 4
        return xx, yy, dev(xx, yy, z, core)

    def slot_of(dz):
        return ((z + dz + 8) % 8) * 2 + core

    own = slot_of(0)

    loads = [
        pltpu.make_async_copy(gc_hbm.at[0], G.at[own], load_sem.at[0]),
        pltpu.make_async_copy(uc_hbm.at[0], U.at[own], load_sem.at[1]),
    ]
    for j in range(NJ):
        loads.append(
            pltpu.make_async_copy(
                dc_hbm.at[0, :, pl.ds(OFFS[j], SUBS[j])], Ds[j].at[own], load_sem.at[2 + j]
            )
        )
    for c in loads:
        c.start()
    hid_loads = [
        pltpu.make_async_copy(
            hid_hbm.at[:, pl.ds(b * BUCKET, BUCKET)], hid_v.at[b], hid_sem.at[b]
        )
        for b in range(NB)
    ]
    for c in hid_loads:
        c.start()

    barrier = pltpu.get_barrier_semaphore()
    for d in (ring_dev[0], ring_dev[1], sib_dev, far_dev):
        pl.semaphore_signal(barrier, inc=1, device_id=d, device_id_type=MESH)

    def greet(d, carry):
        pl.semaphore_signal(barrier, inc=1, device_id=plane_dev(d)[2], device_id_type=MESH)
        return carry

    lax.fori_loop(1, PLANE, greet, 0)

    lane = lax.broadcasted_iota(jnp.int32, (1, 256), 1)

    def scale_gu(buf, scale_ref):
        sc = scale_ref[0].astype(jnp.float32)
        wide = jnp.where(lane < BLOCK, sc[:, 0:1], sc[:, 1:2])
        for r in range(BUCKET // BLOCK):
            rows = pl.ds(r * BLOCK, BLOCK)
            buf[own, rows, :] = (
                buf[own, rows, :].astype(jnp.float32) * wide[r : r + 1, :]
            ).astype(jnp.bfloat16)

    def copy(src, dst, ssem, rsem, device):
        return pltpu.make_async_remote_copy(
            src_ref=src, dst_ref=dst, send_sem=ssem, recv_sem=rsem,
            device_id=device, device_id_type=MESH,
        )

    sends = []

    def start(c):
        c.start()
        sends.append(c)

    GU = (G, U)

    def gu_ring(w, hop, kind):
        s = slot_of(-hop if w == 0 else hop)
        return copy(
            GU[kind].at[s], GU[kind].at[s],
            ring_s.at[w, hop, kind], ring_r.at[w, hop, kind], ring_dev[w],
        )

    def gu_arrived(w, hop, kind):
        s = slot_of(-(hop + 1) if w == 0 else hop + 1)
        copy(
            GU[kind].at[s], GU[kind].at[s],
            ring_s.at[w, hop, kind], ring_r.at[w, hop, kind], ring_dev[w],
        ).wait_recv()

    def q_of(w, h):
        return 0 if h == 0 else (7 if h == 4 else (2 * h if w == 0 else 2 * h - 1))

    def gu_sib(w, h, kind):
        s = slot_of(-h if w == 0 else h)
        q = q_of(w, h)
        return copy(
            GU[kind].at[s], GU[kind].at[s], sib_s.at[q, kind], sib_r.at[q, kind], sib_dev
        )

    def gu_sib_arrived(w, h, kind):
        s = ((z + (-h if w == 0 else h) + 8) % 8) * 2 + 1 - core
        q = q_of(w, h)
        copy(
            GU[kind].at[s], GU[kind].at[s], sib_s.at[q, kind], sib_r.at[q, kind], sib_dev
        ).wait_recv()

    def d_part(j, s, w, far):
        if far:
            return Ds[j].at[s, pl.ds(w * 128, 128), :]
        return Ds[j].at[s]

    def d_ring(j, w, hop):
        s = slot_of(-hop if w == 0 else hop)
        ref = d_part(j, s, w, hop == 3)
        return copy(ref, ref, dring_s.at[j, w, hop], dring_r.at[j, w, hop], ring_dev[w])

    def d_arrived(j, w, hop):
        s = slot_of(-(hop + 1) if w == 0 else hop + 1)
        ref = d_part(j, s, w, hop == 3)
        copy(
            ref, ref, dring_s.at[j, w, hop], dring_r.at[j, w, hop], ring_dev[w]
        ).wait_recv()

    def d_sib(j, w, h):
        s = slot_of(-h if w == 0 else h)
        ref = d_part(j, s, w, h == 4)
        q = 8 if (h == 4 and w == 1) else q_of(w, h)
        return copy(ref, ref, dsib_s.at[j, q], dsib_r.at[j, q], sib_dev)

    def d_sib_arrived(j, w, h):
        s = ((z + (-h if w == 0 else h) + 8) % 8) * 2 + 1 - core
        ref = d_part(j, s, w, h == 4)
        q = 8 if (h == 4 and w == 1) else q_of(w, h)
        copy(ref, ref, dsib_s.at[j, q], dsib_r.at[j, q], sib_dev).wait_recv()

    loads[0].wait()
    scale_gu(G, gs_ref)
    pl.semaphore_wait(barrier, PLANE - 1 + 4)
    start(gu_ring(0, 0, 0))
    start(gu_ring(1, 0, 0))
    loads[1].wait()
    scale_gu(U, us_ref)
    start(gu_ring(0, 0, 1))
    start(gu_ring(1, 0, 1))
    start(gu_sib(0, 0, 0))
    start(gu_sib(0, 0, 1))

    owners = jnp.zeros((8, 128), jnp.int32)
    lane8 = lax.broadcasted_iota(jnp.int32, (8, 128), 1)
    for b in range(NB):
        owners = jnp.where(lane8 == b, own_ref[0, b], owners)
    row_tx[...] = owners
    row_copy = copy(row_tx, row_rx, row_s, row_r, far_dev)
    start(row_copy)

    expert_lane = (lane % SLOTS) // CAP
    slot_lane = (lane % CAP).astype(jnp.float32)
    picked = jnp.zeros((TOK, 256), jnp.float32)
    weight = jnp.zeros((TOK, 256), jnp.float32)
    for k in range(8):
        hit = ids_ref[:, k : k + 1] == expert_lane
        picked = jnp.where(hit, 1.0, picked)
        weight = jnp.where(hit, rw_ref[:, k : k + 1], weight)
    row_i = lax.broadcasted_iota(jnp.int32, (TOK, TOK), 0)
    col_i = lax.broadcasted_iota(jnp.int32, (TOK, TOK), 1)
    below = jnp.where(col_i < row_i, 1.0, 0.0).astype(jnp.bfloat16)
    before = jnp.dot(below, picked.astype(jnp.bfloat16), preferred_element_type=jnp.float32)
    place = jnp.where(before == slot_lane, picked, 0.0)
    combine = place * weight
    first = combine.astype(jnp.bfloat16)
    rest = combine - first.astype(jnp.float32)
    second = rest.astype(jnp.bfloat16)
    third = (rest - second.astype(jnp.float32)).astype(jnp.bfloat16)
    group = lane // SLOTS
    comb_ref[...] = jnp.where(
        group == 0,
        first.astype(jnp.float32),
        jnp.where(
            group == 1,
            second.astype(jnp.float32),
            jnp.where(group == 2, third.astype(jnp.float32), 0.0),
        ),
    ).astype(jnp.bfloat16)
    placing = place.T[:SLOTS, :].astype(jnp.bfloat16)

    for b in range(NB):
        hid_loads[b].wait()

    def gather(b, carry):
        S[b] = jnp.dot(placing, hid_v[b], preferred_element_type=jnp.float32).astype(
            jnp.bfloat16
        )
        return carry

    lax.fori_loop(0, NB, gather, 0)

    def rows16(i):
        return pl.ds(pl.multiple_of(i * CAP, CAP), CAP)

    def disp_copy(d, sx, sy):
        return copy(
            S.at[:, rows16(sy), :], X.at[:, rows16(me_xy), :],
            disp_s.at[d], disp_r.at[d], dev(sx, sy, z, core),
        )

    def disp_start(d, carry):
        xx, yy, _ = plane_dev(d)
        disp_copy(d, xx, yy).start()
        return carry

    lax.fori_loop(1, PLANE, disp_start, 0)
    X[:, rows16(me_xy), :] = S[:, rows16(y), :]

    dsc = ds_ref[0].astype(jnp.float32)
    for j in range(NJ):
        loads[2 + j].wait()
        for rb in range(HID // BLOCK):
            for k in range(SUBS[j] // BLOCK):
                cb = OFFS[j] // BLOCK + k
                at = (own, pl.ds(rb * BLOCK, BLOCK), pl.ds(k * BLOCK, BLOCK))
                Ds[j][at] = (
                    Ds[j][at].astype(jnp.float32) * dsc[rb : rb + 1, cb : cb + 1]
                ).astype(jnp.bfloat16)

    def d_own(j):
        start(d_ring(j, 0, 0))
        start(d_ring(j, 1, 0))
        start(d_sib(j, 0, 0))

    def gu_event(h, kind):
        for w in (0, 1):
            if h == 4 and kind != w:
                continue
            gu_arrived(w, h - 1, kind)
            if h < 3 or (h == 3 and kind == w):
                start(gu_ring(w, h, kind))
            start(gu_sib(w, h, kind))

    def d_event(j, h):
        for w in (0, 1):
            d_arrived(j, w, h - 1)
            if h < 4:
                start(d_ring(j, w, h))
            start(d_sib(j, w, h))

    gu_event(1, 0)

    row_copy.wait_recv()
    to_smem = pltpu.make_async_copy(row_rx, row_sm, row_l)
    to_smem.start()
    to_smem.wait()
    for b in range(NB):
        tab_sm[z_hi * NB + b] = own_ref[0, b]
        tab_sm[(1 - z_hi) * NB + b] = row_sm[0, b]
    for g in range(NB):
        mine, theirs = jnp.int32(0), jnp.int32(0)
        for b in range(1, NB):
            mine = jnp.where(own_ref[0, b] == g, b, mine)
            theirs = jnp.where(row_sm[0, b] == g, b, theirs)
        inv_sm[z_hi * NB + g] = mine
        inv_sm[(1 - z_hi) * NB + g] = theirs

    gu_event(1, 1)
    gu_event(2, 0)
    gu_event(2, 1)
    d_own(0)
    gu_event(3, 0)

    def disp_wait(d, carry):
        disp_copy(d, x, y).wait_recv()
        return carry

    lax.fori_loop(1, PLANE, disp_wait, 0)

    acc[...] = jnp.zeros_like(acc)

    def gu_block(r, carry):
        q = r // 2
        k = (q + 1) // 2
        zz = (z + k * (1 - 2 * ((q + 1) % 2)) + 8) % 8
        s = zz * 2 + (core + r) % 2
        p = zz // 4
        xb = X[inv_sm[s]]
        acc[p, 0] += jnp.dot(xb, G[s], preferred_element_type=jnp.float32)
        acc[p, 1] += jnp.dot(xb, U[s], preferred_element_type=jnp.float32)
        return carry

    for h in range(3):
        for w in (0, 1):
            if h == 0 and w == 1:
                continue
            gu_sib_arrived(w, h, 0)
            gu_sib_arrived(w, h, 1)
    lax.fori_loop(0, 10, gu_block, 0)

    gu_event(3, 1)
    d_event(0, 1)
    d_own(1)
    gu_event(4, 0)
    gu_event(4, 1)
    for w in (0, 1):
        gu_sib_arrived(w, 3, 0)
        gu_sib_arrived(w, 3, 1)
    lax.fori_loop(10, 14, gu_block, 0)
    d_event(0, 2)
    d_event(1, 1)
    gu_sib_arrived(0, 4, 0)
    gu_sib_arrived(1, 4, 1)
    lax.fori_loop(14, 16, gu_block, 0)
    for p in (0, 1):
        H[:, p * HID : (p + 1) * HID] = (jax.nn.silu(acc[p, 0]) * acc[p, 1]).astype(jnp.bfloat16)

    def ret_copy(j, d, xx, yy):
        return copy(
            Ps[j].at[:, rows16(yy * 4 + xx), :], Rs[j].at[:, rows16(x * 4 + y), :],
            ret_s.at[j, d], ret_r.at[j, d], dev(xx, yy, z, core),
        )

    def down(j):
        for h in range(5):
            for w in (0, 1):
                if h == 0 and w == 1:
                    continue
                d_sib_arrived(j, w, h)

        def one(b, carry):
            out = jnp.dot(
                H[:, :HID], Ds[j][tab_sm[b]], preferred_element_type=jnp.float32
            ) + jnp.dot(
                H[:, HID:], Ds[j][NB + tab_sm[NB + b]], preferred_element_type=jnp.float32
            )
            Ps[j][b] = out.astype(jnp.bfloat16)
            return carry

        lax.fori_loop(0, NB, one, 0)

        def send(d, carry):
            xx, yy, _ = plane_dev(d)
            ret_copy(j, d, xx, yy).start()
            return carry

        lax.fori_loop(1, PLANE, send, 0)
        Rs[j][:, rows16(x * 4 + y), :] = Ps[j][:, rows16(me_xy), :]

    def finish(j):
        def arrive(d, carry):
            ret_copy(j, d, x, y).wait_recv()
            return carry

        lax.fori_loop(1, PLANE, arrive, 0)
        for b in range(NB):
            total = Rs[j][b, 0:SLOTS, :].astype(jnp.float32)
            for xx in range(1, 4):
                total = total + Rs[j][b, xx * SLOTS : (xx + 1) * SLOTS, :].astype(jnp.float32)
            es_ref[:, b * BUCKET + OFFS[j] : b * BUCKET + OFFS[j] + SUBS[j]] = total.astype(
                jnp.bfloat16
            )

    d_event(0, 3)
    d_event(1, 2)
    d_own(2)
    d_event(0, 4)
    d_event(1, 3)
    down(0)
    d_event(2, 1)
    d_own(3)
    d_event(1, 4)
    d_event(2, 2)
    down(1)
    d_event(3, 1)
    d_event(2, 3)
    d_event(3, 2)
    d_event(2, 4)
    d_event(3, 3)
    down(2)
    d_event(3, 4)
    down(3)
    for j in range(NJ):
        finish(j)

    for c in sends:
        c.wait_send()

    def sent(d, carry):
        disp_copy(d, x, y).wait_send()
        for j in range(NJ):
            ret_copy(j, d, x, y).wait_send()
        return carry

    lax.fori_loop(1, PLANE, sent, 0)


def mix_kernel(comb_ref, es_ref, out_ref):
    es = es_ref[...]
    out_ref[...] = jnp.dot(
        comb_ref[...], jnp.concatenate([es, es, es, es], axis=0),
        preferred_element_type=jnp.float32,
    ).astype(jnp.bfloat16)


def on_device(
    hidden_in, expert_ids, route_weight, gate_codes, gate_scales, up_codes, up_scales,
    down_codes, down_scales, bucket_owner,
):
    vmem = pl.BlockSpec(memory_space=pltpu.VMEM)
    smem = pl.BlockSpec(memory_space=pltpu.SMEM)
    anys = pl.BlockSpec(memory_space=pl.ANY)
    dma = pltpu.SemaphoreType.DMA
    bf16 = jnp.bfloat16
    es, comb = pl.pallas_call(
        kernel,
        out_shape=(
            jax.ShapeDtypeStruct((SLOTS, D), bf16),
            jax.ShapeDtypeStruct((TOK, 256), bf16),
        ),
        in_specs=[anys, vmem, vmem, anys, anys, anys, vmem, vmem, vmem, smem],
        out_specs=(vmem, vmem),
        scratch_shapes=[
            pltpu.VMEM((16, BUCKET, HID), bf16),
            pltpu.VMEM((16, BUCKET, HID), bf16),
            [pltpu.VMEM((16, HID, s), bf16) for s in SUBS],
            pltpu.VMEM((NB, ROWS, BUCKET), bf16),
            pltpu.VMEM((NB, SLOTS, BUCKET), bf16),
            pltpu.VMEM((NB, TOK, BUCKET), bf16),
            pltpu.VMEM((2, 2, ROWS, HID), jnp.float32),
            pltpu.VMEM((ROWS, 2 * HID), bf16),
            [pltpu.VMEM((NB, ROWS, s), bf16) for s in SUBS],
            [pltpu.VMEM((NB, ROWS, s), bf16) for s in SUBS],
            pltpu.VMEM((8, 128), jnp.int32),
            pltpu.VMEM((8, 128), jnp.int32),
            pltpu.SMEM((8, 128), jnp.int32),
            pltpu.SMEM((16,), jnp.int32),
            pltpu.SMEM((16,), jnp.int32),
            dma((2 + NJ,)),
            dma((NB,)),
            dma((2, 4, 2)),
            dma((2, 4, 2)),
            dma((NJ, 2, 4)),
            dma((NJ, 2, 4)),
            dma((8, 2)),
            dma((8, 2)),
            dma((NJ, 9)),
            dma((NJ, 9)),
            dma((PLANE,)),
            dma((PLANE,)),
            dma((NJ, PLANE)),
            dma((NJ, PLANE)),
            dma(()),
            dma(()),
            dma(()),
        ],
        compiler_params=pltpu.CompilerParams(
            collective_id=0, has_side_effects=True, vmem_limit_bytes=56 * 1024 * 1024
        ),
        name="experts",
    )(
        hidden_in, expert_ids, route_weight, gate_codes, up_codes, down_codes,
        gate_scales, up_scales, down_scales, bucket_owner,
    )
    tile = 1024
    return pl.pallas_call(
        mix_kernel,
        grid=(D // tile,),
        out_shape=jax.ShapeDtypeStruct((TOK, D), bf16),
        in_specs=[
            pl.BlockSpec((TOK, 256), lambda i: (0, 0)),
            pl.BlockSpec((SLOTS, tile), lambda i: (0, i)),
        ],
        out_specs=pl.BlockSpec((TOK, tile), lambda i: (0, i)),
        name="mix",
    )(comb, es)


def solution(mesh):
    tokens = P(("engine", "ep"), None)
    in_specs = (
        tokens,
        tokens,
        tokens,
        P("ep", "engine", None),
        P("ep", "engine", None),
        P("ep", "engine", None),
        P("ep", "engine", None),
        P("ep", None, "engine"),
        P("ep", None, "engine"),
        P("ep", None),
    )
    return jax.shard_map(
        on_device, mesh=mesh, in_specs=in_specs, out_specs=tokens, check_vma=False
    )
```

time: 749 us -> 166 us (0.22)
  the two profiles are of different devices: /device:TPU:2 before, /device:TPU:1 now
where the time goes in v1:
time: 166 us; the launch traced here: 165 us
  Pallas kernels  160 us (96%)
  local copies, waits for them, and re-layouts  5.59 us (3%)
    pallas_call x1, Pallas kernels, on_device(): pl.pallas_call(kernel, out_shape=(jax.ShapeDtypeStruct((SLOTS, D), bf16),...  154 us
    pallas_call x1, Pallas kernels, on_device(): pl.pallas_call(mix_kernel, grid=(D // tile,), out_shape=jax.ShapeDtypeStr...  6.25 us
    unnamed x4, local copies, waits for them, and re-layouts  5.59 us

profile of v1, /device:TPU:1, one launch (start us, length us, event | category | flops | bytes accessed | tf_op | source)
XLA Modules:
  0.0 165.4 jit_solution(16277949577219393075)
XLA Ops:
  0.0 1.3 copy.13.gs_ref
  1.3 1.3 copy.14.us_ref
  2.6 1.5 copy.11.ids_ref
  4.1 1.5 copy.12.rw_ref
  5.6 153.6 %experts.1 = (bf16[64,7168]{1,0:T(8,128)(2,1)}, bf16[256,256]{1,0:T(8,128)(2,1)}) custom-call(bf16[256,7168]{1,0:T(8,128)(2,1)} %hid_hbm.1, s32[256,8]{1,0:T(8,128)} %copy.11.ids_ref, f32[256,8]{1,0:T(8,128)} %copy.12.rw_ref, bf16[1,896,256]{2,1,0:T(8,128)(2,1)} %gc_hbm.1, bf16[1,896,256]{2,1,0:T(8,128)(2,1)} %uc_hbm.1, bf16[1,256,896]{2,1,0:T(8,128)(2,1)} %dc_hbm.1, ...), custom_call_target="tpu_custom_call" | custom-call | tf_op jit(solution)/shard_map/experts/pallas_call | solution.py:447
  159.2 6.2 %mix.1 = bf16[256,7168]{1,0:T(8,128)(2,1)} custom-call(bf16[256,256]{1,0:T(8,128)(2,1)} %get-tuple-element.7.comb_ref, bf16[64,7168]{1,0:T(8,128)(2,1)} %get-tuple-element.8.es_ref), custom_call_target="tpu_custom_call" | custom-call | tf_op jit(solution)/shard_map/mix/pallas_call | solution.py:498

commit v2 on v1

v2 whole, which is shorter than its diff:
```python
import jax
import jax.numpy as jnp
from jax import lax
from jax.experimental import pallas as pl
from jax.experimental.pallas import tpu as pltpu
from jax.sharding import PartitionSpec as P

D = 7168
BLOCK = 128
CAP = 16
NB = 8
BUCKET = D // NB
HALF = BUCKET // 2
HID = 256
TOK = 256
LIVE = 4
SLOTS = LIVE * CAP
PLANE = 16
ROWS = PLANE * CAP
SUB = 128
NJ = BUCKET // SUB
FROM = 3 * SLOTS
MESH = pl.DeviceIdType.MESH

SPREAD = (
    (1, 0), (0, 1), (3, 0), (0, 3), (1, 1), (3, 3), (2, 0), (0, 2),
    (1, 3), (3, 1), (2, 1), (1, 2), (2, 3), (3, 2), (2, 2),
)


def kernel(
    hid_hbm, ids_ref, rw_ref, gc_hbm, uc_hbm, dc_hbm, gs_ref, us_ref, ds_ref, own_ref,
    es_ref, comb_ref,
    G, U, Ds, X, S, hid_v, acc, H, Ps, As, Rs, row_tx, row_rx, row_sm, inv_sm, tab_sm,
    load_sem, hid_sem, gu_s, ring_r, d_s, dring_r, gsib_s, sib_r, dsib_s, dsib_r,
    disp_s, disp_r, ret_s, ret_ra, ret_r, row_s, row_r, row_l,
):
    eng = lax.axis_index("engine")
    ep = lax.axis_index("ep")
    z_lo, core = eng // 2, eng % 2
    x, z_hi, y = ep % 4, (ep // 4) % 2, ep // 8
    z = z_hi * 4 + z_lo
    me_xy = x * 4 + y
    x_right, x_left, x_far = (x + 1) % 4, (x + 3) % 4, (x + 2) % 4

    def dev(xx, yy, zz, cc):
        return ((zz % 4) * 2 + cc, (yy * 2 + zz // 4) * 4 + xx)

    ring_dev = (dev(x, y, (z + 1) % 8, core), dev(x, y, (z + 7) % 8, core))
    sib_dev = dev(x, y, z, 1 - core)
    far_dev = dev(x, y, (z + 4) % 8, core)

    def plane(xx, yy):
        return dev(xx, yy, z, core)

    def at(w, h, cc):
        return ((z + (8 - h if w == 0 else h)) % 8) * 2 + cc

    own = at(0, 0, core)

    loads = [
        pltpu.make_async_copy(gc_hbm.at[0], G.at[own], load_sem.at[0]),
        pltpu.make_async_copy(uc_hbm.at[0], U.at[own], load_sem.at[1]),
    ]
    for j in range(NJ):
        loads.append(
            pltpu.make_async_copy(
                dc_hbm.at[0, :, pl.ds(j * SUB, SUB)], Ds[j].at[own], load_sem.at[2 + j]
            )
        )
    for c in loads[:2]:
        c.start()

    barrier = pltpu.get_barrier_semaphore()
    greeted = [ring_dev[0], ring_dev[1], sib_dev, far_dev]
    greeted += [plane((x + dx) % 4, (y + dy) % 4) for dx, dy in SPREAD]
    for d in greeted:
        pl.semaphore_signal(barrier, inc=1, device_id=d, device_id_type=MESH)

    hid_loads = [
        pltpu.make_async_copy(
            hid_hbm.at[:, pl.ds(b * BUCKET, BUCKET)], hid_v.at[b], hid_sem.at[b]
        )
        for b in range(NB)
    ]
    for c in hid_loads + loads[2:]:
        c.start()

    def scale_gu(buf, scale_ref):
        sc = scale_ref[0].astype(jnp.float32)
        for r in range(BUCKET // BLOCK):
            for cb in range(HID // BLOCK):
                i = (own, pl.ds(r * BLOCK, BLOCK), pl.ds(cb * BLOCK, BLOCK))
                buf[i] = (
                    buf[i].astype(jnp.float32) * sc[cb : cb + 1, r : r + 1]
                ).astype(jnp.bfloat16)

    def copy(src, dst, ssem, rsem, device):
        return pltpu.make_async_remote_copy(
            src_ref=src, dst_ref=dst, send_sem=ssem, recv_sem=rsem,
            device_id=device, device_id_type=MESH,
        )

    GU = (G, U)

    def gu_part(kind, w, h, cc):
        s = at(w, h, cc)
        if h == 4:
            return GU[kind].at[s, pl.ds(w * HALF, HALF), :]
        return GU[kind].at[s]

    def gu_ring(kind, w, hop):
        s = at(w, hop, core)
        ref = GU[kind].at[s, pl.ds(w * HALF, HALF), :] if hop == 3 else GU[kind].at[s]
        return copy(ref, ref, gu_s.at[kind], ring_r.at[kind, w, hop], ring_dev[w])

    def gu_arrived(kind, w, h):
        ref = gu_part(kind, w, h, core)
        copy(ref, ref, gu_s.at[kind], ring_r.at[kind, w, h - 1], ring_dev[w]).wait_recv()

    def gu_sib(kind, w, h, cc):
        ref = gu_part(kind, w, h, cc)
        return copy(ref, ref, gsib_s.at[kind], sib_r.at[kind, w, h], sib_dev)

    def d_part(j, w, h, cc):
        s = at(w, h, cc)
        if h == 4:
            return Ds[j].at[s, pl.ds(w * BLOCK, BLOCK), :]
        return Ds[j].at[s]

    def d_ring(j, w, hop):
        s = at(w, hop, core)
        ref = Ds[j].at[s, pl.ds(w * BLOCK, BLOCK), :] if hop == 3 else Ds[j].at[s]
        return copy(ref, ref, d_s.at[j], dring_r.at[j, w, hop], ring_dev[w])

    def d_arrived(j, w, h):
        ref = d_part(j, w, h, core)
        copy(ref, ref, d_s.at[j], dring_r.at[j, w, h - 1], ring_dev[w]).wait_recv()

    def d_sib(j, w, h):
        ref = d_part(j, w, h, core)
        return copy(ref, ref, dsib_s.at[j], dsib_r.at[j], sib_dev)

    def gu_event(kind, h):
        for w in (0, 1):
            gu_arrived(kind, w, h)
            if h < 4:
                gu_ring(kind, w, h).start()
            gu_sib(kind, w, h, core).start()

    def gu_sib_wait(kind, h):
        for w in (0, 1):
            if h > 0 or w == 0:
                gu_sib(kind, w, h, 1 - core).wait_recv()

    def d_own(j):
        d_ring(j, 0, 0).start()
        d_ring(j, 1, 0).start()
        d_sib(j, 0, 0).start()

    def d_event(j, h):
        for w in (0, 1):
            d_arrived(j, w, h)
            if h < 4:
                d_ring(j, w, h).start()
            d_sib(j, w, h).start()

    loads[0].wait()
    scale_gu(G, gs_ref)
    pl.semaphore_wait(barrier, len(greeted))
    gu_ring(0, 0, 0).start()
    gu_ring(0, 1, 0).start()
    loads[1].wait()
    scale_gu(U, us_ref)
    gu_ring(1, 0, 0).start()
    gu_ring(1, 1, 0).start()
    gu_sib(0, 0, 0, core).start()
    gu_sib(1, 0, 0, core).start()

    slot = lax.broadcasted_iota(jnp.int32, (SLOTS, 1), 0)
    expert_of = slot // CAP
    place_of = (slot % CAP).astype(jnp.float32)
    picked = jnp.zeros((SLOTS, TOK), jnp.float32)
    weight = jnp.zeros((SLOTS, TOK), jnp.float32)
    for k in range(8):
        hit = ids_ref[k : k + 1, :] == expert_of
        picked = jnp.where(hit, 1.0, picked)
        weight = jnp.where(hit, rw_ref[k : k + 1, :], weight)
    row_i = lax.broadcasted_iota(jnp.int32, (TOK, TOK), 0)
    col_i = lax.broadcasted_iota(jnp.int32, (TOK, TOK), 1)
    earlier = jnp.where(row_i < col_i, 1.0, 0.0).astype(jnp.bfloat16)
    before = jnp.dot(picked.astype(jnp.bfloat16), earlier, preferred_element_type=jnp.float32)
    place = jnp.where(before == place_of, picked, 0.0)
    placing = place.astype(jnp.bfloat16)

    for b in range(NB):
        hid_loads[b].wait()
        S[b] = jnp.dot(placing, hid_v[b], preferred_element_type=jnp.float32).astype(
            jnp.bfloat16
        )

    def rows16(i):
        return pl.ds(pl.multiple_of(i * CAP, CAP), CAP)

    for dx, dy in SPREAD:
        xx, yy = (x + dx) % 4, (y + dy) % 4
        copy(
            S.at[:, rows16(yy), :], X.at[:, rows16(me_xy), :], disp_s, disp_r, plane(xx, yy)
        ).start()
    X[:, rows16(me_xy), :] = S[:, rows16(y), :]

    owners = jnp.zeros((8, 128), jnp.int32)
    lane8 = lax.broadcasted_iota(jnp.int32, (8, 128), 1)
    for b in range(NB):
        owners = jnp.where(lane8 == b, own_ref[0, b], owners)
    row_tx[...] = owners
    row_copy = copy(row_tx, row_rx, row_s, row_r, far_dev)
    row_copy.start()

    dsc = ds_ref[0].astype(jnp.float32)
    for j in range(NJ):
        loads[2 + j].wait()
        for rb in range(HID // BLOCK):
            i = (own, pl.ds(rb * BLOCK, BLOCK), slice(None))
            Ds[j][i] = (
                Ds[j][i].astype(jnp.float32) * dsc[rb : rb + 1, j : j + 1]
            ).astype(jnp.bfloat16)

    gu_event(0, 1)

    combine = place * weight
    first = combine.astype(jnp.bfloat16).astype(jnp.float32)
    second = (combine - first).astype(jnp.bfloat16).astype(jnp.float32)
    third = combine - first - second
    stacked = jnp.concatenate([first, second, third, jnp.zeros_like(third)], axis=0)
    comb_ref[...] = stacked.T.astype(jnp.bfloat16)

    row_copy.wait_recv()
    to_smem = pltpu.make_async_copy(row_rx, row_sm, row_l)
    to_smem.start()
    to_smem.wait()
    for b in range(NB):
        tab_sm[z_hi * NB + b] = own_ref[0, b]
        tab_sm[(1 - z_hi) * NB + b] = row_sm[0, b]
    for g in range(NB):
        mine, theirs = jnp.int32(0), jnp.int32(0)
        for b in range(1, NB):
            mine = jnp.where(own_ref[0, b] == g, b, mine)
            theirs = jnp.where(row_sm[0, b] == g, b, theirs)
        inv_sm[z_hi * NB + g] = mine
        inv_sm[(1 - z_hi) * NB + g] = theirs
    acc[...] = jnp.zeros_like(acc)

    def gu_block(r, carry):
        q = r // 2
        k = (q + 1) // 2
        zz = (z + k * (1 - 2 * ((q + 1) % 2)) + 8) % 8
        s = zz * 2 + (core + r) % 2
        p = zz // 4
        xb = X[inv_sm[s]]
        acc[p, 0] += jnp.dot(xb, G[s], preferred_element_type=jnp.float32)
        acc[p, 1] += jnp.dot(xb, U[s], preferred_element_type=jnp.float32)
        return carry

    def gu_blocks(lo, hi):
        lax.fori_loop(lo, hi, gu_block, 0)

    def rows(xx, yy):
        return rows16(xx * 4 + yy)

    def ret_copy(j, xx, yy, part):
        return copy(
            Ps[j].at[:, rows(xx, yy), :], Rs[j].at[:, rows(part, y), :],
            ret_s.at[j], ret_r.at[j], plane(xx, yy),
        )

    def down(j):
        copy(
            Ds[j].at[pl.ds(0, 8)], Ds[j].at[pl.ds(0, 8)], dsib_s.at[j], dsib_r.at[j], sib_dev
        ).wait_recv()
        for b in range(0, NB, 2):
            near = jnp.concatenate([Ds[j][tab_sm[b]], Ds[j][tab_sm[b + 1]]], axis=1)
            far = jnp.concatenate(
                [Ds[j][NB + tab_sm[NB + b]], Ds[j][NB + tab_sm[NB + b + 1]]], axis=1
            )
            out = jnp.dot(H[:, :HID], near, preferred_element_type=jnp.float32) + jnp.dot(
                H[:, HID:], far, preferred_element_type=jnp.float32
            )
            Ps[j][b] = out[:, :SUB].astype(jnp.bfloat16)
            Ps[j][b + 1] = out[:, SUB:].astype(jnp.bfloat16)
        for w, xx in ((0, x_right), (1, x_left)):
            some = pl.ds(pl.multiple_of(x_far * SLOTS + w * 32, 32), 32)
            copy(
                Ps[j].at[:, some, :], As[j].at[w], ret_s.at[j], ret_ra.at[j], plane(xx, y)
            ).start()
        for k in (0, 1):
            ret_copy(j, x_right, 2 + k, 1).start()
            ret_copy(j, x_left, k, 2).start()
        for dy in (1, 3, 2):
            ret_copy(j, x, (y + dy) % 4, 0).start()
        Rs[j][:, rows(0, y), :] = Ps[j][:, rows(x, y), :]

    def relay(j):
        copy(As[j], As[j], ret_s.at[j], ret_ra.at[j], sib_dev).wait_recv()
        for w, xx in ((0, x_right), (1, x_left)):
            some = pl.ds(pl.multiple_of(xx * SLOTS + w * 32, 32), 32)
            Ps[j][:, some, :] = (
                Ps[j][:, some, :].astype(jnp.float32) + As[j][w].astype(jnp.float32)
            ).astype(jnp.bfloat16)
        for k in (0, 1):
            ret_copy(j, x_right, k, 1).start()
            ret_copy(j, x_left, 2 + k, 2).start()

    def finish(j):
        got = Rs[j].at[:, pl.ds(0, 11 * CAP), :]
        copy(got, got, ret_s.at[j], ret_r.at[j], sib_dev).wait_recv()
        for b in range(NB):
            total = Rs[j][b, 0:SLOTS, :].astype(jnp.float32)
            for part in (1, 2):
                total = total + Rs[j][b, part * SLOTS : (part + 1) * SLOTS, :].astype(
                    jnp.float32
                )
            es_ref[:, b * BUCKET + j * SUB : b * BUCKET + (j + 1) * SUB] = total.astype(
                jnp.bfloat16
            )

    gu_event(1, 1)
    gu_event(0, 2)
    d_own(0)
    gu_event(1, 2)
    got = X.at[:, pl.ds(0, ROWS - CAP), :]
    copy(got, got, disp_s, disp_r, sib_dev).wait_recv()
    for h in (0, 1):
        for kind in (0, 1):
            gu_sib_wait(kind, h)
    gu_blocks(0, 6)
    d_event(0, 1)
    d_own(1)
    gu_event(0, 3)
    for kind in (0, 1):
        gu_sib_wait(kind, 2)
    gu_blocks(6, 10)
    d_event(0, 2)
    d_event(1, 1)
    gu_event(0, 4)
    gu_event(1, 3)
    for kind in (0, 1):
        gu_sib_wait(kind, 3)
    gu_blocks(10, 14)
    d_event(0, 3)
    d_event(1, 2)
    d_own(2)
    gu_event(1, 4)
    for kind in (0, 1):
        gu_sib_wait(kind, 4)
    gu_blocks(14, 16)
    for p in (0, 1):
        H[:, p * HID : (p + 1) * HID] = (jax.nn.silu(acc[p, 0]) * acc[p, 1]).astype(jnp.bfloat16)
    d_event(0, 4)
    d_event(1, 3)
    d_own(3)
    d_event(2, 1)
    down(0)
    d_event(3, 1)
    d_event(1, 4)
    d_event(2, 2)
    d_own(4)
    down(1)
    d_event(2, 3)
    relay(0)
    d_event(3, 2)
    d_event(4, 1)
    d_event(2, 4)
    relay(1)
    d_event(3, 3)
    d_own(5)
    down(2)
    finish(0)
    d_event(4, 2)
    d_event(5, 1)
    d_event(3, 4)
    relay(2)
    finish(1)
    d_event(4, 3)
    d_own(6)
    down(3)
    d_event(5, 2)
    relay(3)
    finish(2)
    d_event(6, 1)
    d_event(4, 4)
    down(4)
    d_event(5, 3)
    d_event(6, 2)
    d_event(5, 4)
    down(5)
    relay(4)
    finish(3)
    d_event(6, 3)
    d_event(6, 4)
    down(6)
    relay(5)
    finish(4)
    relay(6)
    finish(5)

    for kind in (0, 1):
        some = GU[kind].at[pl.ds(0, 7)]
        copy(some, some, gu_s.at[kind], ring_r.at[kind, 0, 0], sib_dev).wait_send()
        some = GU[kind].at[pl.ds(0, 8)]
        copy(some, some, gsib_s.at[kind], ring_r.at[kind, 0, 0], sib_dev).wait_send()
    copy(got, got, disp_s, disp_r, sib_dev).wait_send()
    row_copy.wait_send()
    for j in range(NJ):
        some = Ds[j].at[pl.ds(0, 7)]
        copy(some, some, d_s.at[j], dsib_r.at[j], sib_dev).wait_send()
        some = Ds[j].at[pl.ds(0, 8)]
        copy(some, some, dsib_s.at[j], dsib_r.at[j], sib_dev).wait_send()
    finish(6)
    for j in range(NJ):
        some = Ps[j].at[:, pl.ds(0, 2 * 32 + 11 * CAP), :]
        copy(some, some, ret_s.at[j], ret_r.at[j], sib_dev).wait_send()


TILES = 4
TILE = D // TILES


def mix_kernel(comb_hbm, es_hbm, out_hbm, comb_v, es_v, out_v, comb_sem, es_sem, out_sem):
    comb_load = pltpu.make_async_copy(comb_hbm, comb_v, comb_sem)
    comb_load.start()

    def cols(i):
        return pl.ds(i * TILE, TILE)

    es_loads = [
        pltpu.make_async_copy(es_hbm.at[:, cols(i)], es_v.at[:, cols(i)], es_sem.at[i])
        for i in range(TILES)
    ]
    for c in es_loads:
        c.start()
    comb_load.wait()
    stores = []
    for i in range(TILES):
        es_loads[i].wait()
        es = es_v[:, cols(i)]
        out_v[:, cols(i)] = jnp.dot(
            comb_v[...], jnp.concatenate([es, es, es, es], axis=0),
            preferred_element_type=jnp.float32,
        ).astype(jnp.bfloat16)
        stores.append(
            pltpu.make_async_copy(out_v.at[:, cols(i)], out_hbm.at[:, cols(i)], out_sem.at[i])
        )
        stores[-1].start()
    for c in stores:
        c.wait()


def on_device(
    hidden_in, expert_ids, route_weight, gate_codes, gate_scales, up_codes, up_scales,
    down_codes, down_scales, bucket_owner,
):
    vmem = pl.BlockSpec(memory_space=pltpu.VMEM)
    smem = pl.BlockSpec(memory_space=pltpu.SMEM)
    anys = pl.BlockSpec(memory_space=pl.ANY)
    dma = pltpu.SemaphoreType.DMA
    bf16 = jnp.bfloat16
    es, comb = pl.pallas_call(
        kernel,
        out_shape=(
            jax.ShapeDtypeStruct((SLOTS, D), bf16),
            jax.ShapeDtypeStruct((TOK, 256), bf16),
        ),
        in_specs=[anys, vmem, vmem, anys, anys, anys, vmem, vmem, vmem, smem],
        out_specs=(vmem, vmem),
        scratch_shapes=[
            pltpu.VMEM((16, BUCKET, HID), bf16),
            pltpu.VMEM((16, BUCKET, HID), bf16),
            [pltpu.VMEM((16, HID, SUB), bf16) for _ in range(NJ)],
            pltpu.VMEM((NB, ROWS, BUCKET), bf16),
            pltpu.VMEM((NB, SLOTS, BUCKET), bf16),
            pltpu.VMEM((NB, TOK, BUCKET), bf16),
            pltpu.VMEM((2, 2, ROWS, HID), jnp.float32),
            pltpu.VMEM((ROWS, 2 * HID), bf16),
            [pltpu.VMEM((NB, ROWS, SUB), bf16) for _ in range(NJ)],
            [pltpu.VMEM((2, NB, 32, SUB), bf16) for _ in range(NJ)],
            [pltpu.VMEM((NB, FROM, SUB), bf16) for _ in range(NJ)],
            pltpu.VMEM((8, 128), jnp.int32),
            pltpu.VMEM((8, 128), jnp.int32),
            pltpu.SMEM((8, 128), jnp.int32),
            pltpu.SMEM((16,), jnp.int32),
            pltpu.SMEM((16,), jnp.int32),
            dma((2 + NJ,)),
            dma((NB,)),
            dma((2,)),
            dma((2, 2, 4)),
            dma((NJ,)),
            dma((NJ, 2, 4)),
            dma((2,)),
            dma((2, 2, 5)),
            dma((NJ,)),
            dma((NJ,)),
            dma(()),
            dma(()),
            dma((NJ,)),
            dma((NJ,)),
            dma((NJ,)),
            dma(()),
            dma(()),
            dma(()),
        ],
        compiler_params=pltpu.CompilerParams(
            collective_id=0, has_side_effects=True, vmem_limit_bytes=56 * 1024 * 1024
        ),
        name="experts",
    )(
        hidden_in, expert_ids.T, route_weight.T, gate_codes, up_codes, down_codes,
        gate_scales.transpose(0, 2, 1), up_scales.transpose(0, 2, 1), down_scales, bucket_owner,
    )
    return pl.pallas_call(
        mix_kernel,
        out_shape=jax.ShapeDtypeStruct((TOK, D), bf16),
        in_specs=[anys, anys],
        out_specs=anys,
        scratch_shapes=[
            pltpu.VMEM((TOK, 256), bf16),
            pltpu.VMEM((SLOTS, D), bf16),
            pltpu.VMEM((TOK, D), bf16),
            dma(()),
            dma((TILES,)),
            dma((TILES,)),
        ],
        compiler_params=pltpu.CompilerParams(vmem_limit_bytes=56 * 1024 * 1024),
        name="mix",
    )(comb, es)


def solution(mesh):
    tokens = P(("engine", "ep"), None)
    in_specs = (
        tokens,
        tokens,
        tokens,
        P("ep", "engine", None),
        P("ep", "engine", None),
        P("ep", "engine", None),
        P("ep", "engine", None),
        P("ep", None, "engine"),
        P("ep", None, "engine"),
        P("ep", None),
    )
    return jax.shard_map(
        on_device, mesh=mesh, in_specs=in_specs, out_specs=tokens, check_vma=False
    )
```

time: 166 us -> 144 us (0.87)
  Pallas kernels: 160 us -> 144 us
  local copies, waits for them, and re-layouts: 5.59 us -> 0 us
    pallas_call x1, Pallas kernels: 154 us -> 140 us  [on_device(): pl.pallas_call(kernel, out_shape=(jax.ShapeDtypeStruct((SLOTS, D), bf16),...]
    unnamed x4 -> x0, local copies, waits for them, and re-layouts: 5.59 us -> none
    pallas_call x1, Pallas kernels: 6.25 us -> 4.03 us  [on_device(): pl.pallas_call(mix_kernel, out_shape=jax.ShapeDtypeStruct((TOK, D), bf16)...]
where the time goes in v2:
time: 144 us
  Pallas kernels  144 us (100%)
    pallas_call x1, Pallas kernels, on_device(): pl.pallas_call(kernel, out_shape=(jax.ShapeDtypeStruct((SLOTS, D), bf16),...  140 us
    pallas_call x1, Pallas kernels, on_device(): pl.pallas_call(mix_kernel, out_shape=jax.ShapeDtypeStruct((TOK, D), bf16)...  4.03 us

profile of v2, /device:TPU:1, one launch (start us, length us, event | category | flops | bytes accessed | tf_op | source)
XLA Modules:
  0.0 143.7 jit_solution(5319834719545579502)
XLA Ops:
  0.0 139.7 %experts.1 = (bf16[64,7168]{1,0:T(8,128)(2,1)}, bf16[256,256]{1,0:T(8,128)(2,1)}) custom-call(bf16[256,7168]{1,0:T(8,128)(2,1)} %hid_hbm.1, s32[8,256]{1,0:T(8,128)} %bitcast.4, f32[8,256]{1,0:T(8,128)} %bitcast.5, bf16[1,896,256]{2,1,0:T(8,128)(2,1)} %gc_hbm.1, bf16[1,896,256]{2,1,0:T(8,128)(2,1)} %uc_hbm.1, bf16[1,256,896]{2,1,0:T(8,128)(2,1)} %dc_hbm.1, ...), custom_call_target="tpu_custom_call" | custom-call | tf_op jit(solution)/shard_map/experts/pallas_call | solution.py:468
  139.7 4.0 %mix.1 = bf16[256,7168]{1,0:T(8,128)(2,1)} custom-call(bf16[256,256]{1,0:T(8,128)(2,1)} %get-tuple-element.7.comb_hbm, bf16[64,7168]{1,0:T(8,128)(2,1)} %get-tuple-element.8.es_hbm), custom_call_target="tpu_custom_call" | custom-call | tf_op jit(solution)/shard_map/mix/pallas_call | solution.py:520

commit v3 on v2

--- a/solution.py
+++ b/solution.py
@@ -27,11 +27,33 @@
     (1, 3), (3, 1), (2, 1), (1, 2), (2, 3), (3, 2), (2, 2),
 )
 
+PLAN = (
+    "c0 b0 U1 a0",
+    "b1 c1 a1 G1",
+    "a2 U2 B0-2 B2-4",
+    "B4-6 G2 B6-8 B8-10",
+    "U3 G3 b2 c2",
+    "a3 d0 B10-12 B12-14",
+    "U4 G4 b3 e0",
+    "B14-16 c3 a4 H",
+    "d1 f0 Da b4",
+    "e1 c4 Db d2",
+    "g0 Dc Ra e2",
+    "Rb d3 f1 Rc",
+    "e3 g1 d4 f2",
+    "Dd e4 Fa g2",
+    "De f3 Fb Rd",
+    "Fc g3 f4 Re",
+    "Df g4 Fd Dg",
+    "Fe Rf Rg Ff",
+    "Fg",
+)
+
 
 def kernel(
     hid_hbm, ids_ref, rw_ref, gc_hbm, uc_hbm, dc_hbm, gs_ref, us_ref, ds_ref, own_ref,
-    es_ref, comb_ref,
-    G, U, Ds, X, S, hid_v, acc, H, Ps, As, Rs, row_tx, row_rx, row_sm, inv_sm, tab_sm,
+    out_ref,
+    comb, G, U, Ds, X, S, hid_v, acc, H, Ps, As, Rs, row_tx, row_rx, row_sm, inv_sm, tab_sm,
     load_sem, hid_sem, gu_s, ring_r, d_s, dring_r, gsib_s, sib_r, dsib_s, dsib_r,
     disp_s, disp_r, ret_s, ret_ra, ret_r, row_s, row_r, row_l,
 ):
@@ -146,6 +168,7 @@
             gu_arrived(kind, w, h)
             if h < 4:
                 gu_ring(kind, w, h).start()
+        for w in (0, 1):
             gu_sib(kind, w, h, core).start()
 
     def gu_sib_wait(kind, h):
@@ -163,6 +186,7 @@
             d_arrived(j, w, h)
             if h < 4:
                 d_ring(j, w, h).start()
+        for w in (0, 1):
             d_sib(j, w, h).start()
 
     loads[0].wait()
@@ -226,14 +250,12 @@
                 Ds[j][i].astype(jnp.float32) * dsc[rb : rb + 1, j : j + 1]
             ).astype(jnp.bfloat16)
 
-    gu_event(0, 1)
-
     combine = place * weight
     first = combine.astype(jnp.bfloat16).astype(jnp.float32)
     second = (combine - first).astype(jnp.bfloat16).astype(jnp.float32)
     third = combine - first - second
     stacked = jnp.concatenate([first, second, third, jnp.zeros_like(third)], axis=0)
-    comb_ref[...] = stacked.T.astype(jnp.bfloat16)
+    comb[...] = stacked.T.astype(jnp.bfloat16)
 
     row_copy.wait_recv()
     to_smem = pltpu.make_async_copy(row_rx, row_sm, row_l)
@@ -261,9 +283,6 @@
         acc[p, 0] += jnp.dot(xb, G[s], preferred_element_type=jnp.float32)
         acc[p, 1] += jnp.dot(xb, U[s], preferred_element_type=jnp.float32)
         return carry
-
-    def gu_blocks(lo, hi):
-        lax.fori_loop(lo, hi, gu_block, 0)
 
     def rows(xx, yy):
         return rows16(xx * 4 + yy)
@@ -314,95 +333,55 @@
     def finish(j):
         got = Rs[j].at[:, pl.ds(0, 11 * CAP), :]
         copy(got, got, ret_s.at[j], ret_r.at[j], sib_dev).wait_recv()
+        sums = []
         for b in range(NB):
             total = Rs[j][b, 0:SLOTS, :].astype(jnp.float32)
             for part in (1, 2):
                 total = total + Rs[j][b, part * SLOTS : (part + 1) * SLOTS, :].astype(
                     jnp.float32
                 )
-            es_ref[:, b * BUCKET + j * SUB : b * BUCKET + (j + 1) * SUB] = total.astype(
-                jnp.bfloat16
-            )
-
-    gu_event(1, 1)
-    gu_event(0, 2)
-    d_own(0)
-    gu_event(1, 2)
+            sums.append(total.astype(jnp.bfloat16))
+        for b in range(0, NB, 2):
+            pair = jnp.concatenate(sums[b : b + 2], axis=1)
+            mixed = jnp.dot(
+                comb[...], jnp.concatenate([pair] * 4, axis=0),
+                preferred_element_type=jnp.float32,
+            ).astype(jnp.bfloat16)
+            for k in (0, 1):
+                at_col = (b + k) * BUCKET + j * SUB
+                out_ref[:, at_col : at_col + SUB] = mixed[:, k * SUB : (k + 1) * SUB]
+
     got = X.at[:, pl.ds(0, ROWS - CAP), :]
-    copy(got, got, disp_s, disp_r, sib_dev).wait_recv()
-    for h in (0, 1):
-        for kind in (0, 1):
-            gu_sib_wait(kind, h)
-    gu_blocks(0, 6)
-    d_event(0, 1)
-    d_own(1)
-    gu_event(0, 3)
-    for kind in (0, 1):
-        gu_sib_wait(kind, 2)
-    gu_blocks(6, 10)
-    d_event(0, 2)
-    d_event(1, 1)
-    gu_event(0, 4)
-    gu_event(1, 3)
-    for kind in (0, 1):
-        gu_sib_wait(kind, 3)
-    gu_blocks(10, 14)
-    d_event(0, 3)
-    d_event(1, 2)
-    d_own(2)
-    gu_event(1, 4)
-    for kind in (0, 1):
-        gu_sib_wait(kind, 4)
-    gu_blocks(14, 16)
-    for p in (0, 1):
-        H[:, p * HID : (p + 1) * HID] = (jax.nn.silu(acc[p, 0]) * acc[p, 1]).astype(jnp.bfloat16)
-    d_event(0, 4)
-    d_event(1, 3)
-    d_own(3)
-    d_event(2, 1)
-    down(0)
-    d_event(3, 1)
-    d_event(1, 4)
-    d_event(2, 2)
-    d_own(4)
-    down(1)
-    d_event(2, 3)
-    relay(0)
-    d_event(3, 2)
-    d_event(4, 1)
-    d_event(2, 4)
-    relay(1)
-    d_event(3, 3)
-    d_own(5)
-    down(2)
-    finish(0)
-    d_event(4, 2)
-    d_event(5, 1)
-    d_event(3, 4)
-    relay(2)
-    finish(1)
-    d_event(4, 3)
-    d_own(6)
-    down(3)
-    d_event(5, 2)
-    relay(3)
-    finish(2)
-    d_event(6, 1)
-    d_event(4, 4)
-    down(4)
-    d_event(5, 3)
-    d_event(6, 2)
-    d_event(5, 4)
-    down(5)
-    relay(4)
-    finish(3)
-    d_event(6, 3)
-    d_event(6, 4)
-    down(6)
-    relay(5)
-    finish(4)
-    relay(6)
-    finish(5)
+    first_blocks = True
+    for token in " ".join(PLAN).split():
+        name, rest = token[0], token[1:]
+        if name in "GU":
+            kind, h = "GU".index(name), int(rest)
+            gu_event(kind, h)
+        elif name == "B":
+            lo, hi = map(int, rest.split("-"))
+            if first_blocks:
+                first_blocks = False
+                copy(got, got, disp_s, disp_r, sib_dev).wait_recv()
+            if lo == 0 or lo % 4 == 2:
+                for kind in (0, 1):
+                    gu_sib_wait(kind, (lo + 2) // 4)
+            lax.fori_loop(lo, hi, gu_block, 0)
+        elif name == "H":
+            for p in (0, 1):
+                H[:, p * HID : (p + 1) * HID] = (
+                    jax.nn.silu(acc[p, 0]) * acc[p, 1]
+                ).astype(jnp.bfloat16)
+        elif name == "D":
+            down("abcdefg".index(rest))
+        elif name == "R":
+            relay("abcdefg".index(rest))
+        elif name == "F":
+            finish("abcdefg".index(rest))
+        elif rest == "0":
+            d_own("abcdefg".index(name))
+        else:
+            d_event("abcdefg".index(name), int(rest))
 
     for kind in (0, 1):
         some = GU[kind].at[pl.ds(0, 7)]
@@ -416,44 +395,9 @@
         copy(some, some, d_s.at[j], dsib_r.at[j], sib_dev).wait_send()
         some = Ds[j].at[pl.ds(0, 8)]
         copy(some, some, dsib_s.at[j], dsib_r.at[j], sib_dev).wait_send()
-    finish(6)
     for j in range(NJ):
         some = Ps[j].at[:, pl.ds(0, 2 * 32 + 11 * CAP), :]
         copy(some, some, ret_s.at[j], ret_r.at[j], sib_dev).wait_send()
-
-
-TILES = 4
-TILE = D // TILES
-
-
-def mix_kernel(comb_hbm, es_hbm, out_hbm, comb_v, es_v, out_v, comb_sem, es_sem, out_sem):
-    comb_load = pltpu.make_async_copy(comb_hbm, comb_v, comb_sem)
-    comb_load.start()
-
-    def cols(i):
-        return pl.ds(i * TILE, TILE)
-
-    es_loads = [
-        pltpu.make_async_copy(es_hbm.at[:, cols(i)], es_v.at[:, cols(i)], es_sem.at[i])
-        for i in range(TILES)
-    ]
-    for c in es_loads:
-        c.start()
-    comb_load.wait()
-    stores = []
-    for i in range(TILES):
-        es_loads[i].wait()
-        es = es_v[:, cols(i)]
-        out_v[:, cols(i)] = jnp.dot(
-            comb_v[...], jnp.concatenate([es, es, es, es], axis=0),
-            preferred_element_type=jnp.float32,
-        ).astype(jnp.bfloat16)
-        stores.append(
-            pltpu.make_async_copy(out_v.at[:, cols(i)], out_hbm.at[:, cols(i)], out_sem.at[i])
-        )
-        stores[-1].start()
-    for c in stores:
-        c.wait()
 
 
 def on_device(
@@ -465,15 +409,13 @@
     anys = pl.BlockSpec(memory_space=pl.ANY)
     dma = pltpu.SemaphoreType.DMA
     bf16 = jnp.bfloat16
-    es, comb = pl.pallas_call(
+    return pl.pallas_call(
         kernel,
-        out_shape=(
-            jax.ShapeDtypeStruct((SLOTS, D), bf16),
-            jax.ShapeDtypeStruct((TOK, 256), bf16),
-        ),
+        out_shape=pltpu.VMEM((TOK, D), bf16),
         in_specs=[anys, vmem, vmem, anys, anys, anys, vmem, vmem, vmem, smem],
-        out_specs=(vmem, vmem),
+        out_specs=vmem,
         scratch_shapes=[
+            pltpu.VMEM((TOK, 256), bf16),
             pltpu.VMEM((16, BUCKET, HID), bf16),
             pltpu.VMEM((16, BUCKET, HID), bf16),
             [pltpu.VMEM((16, HID, SUB), bf16) for _ in range(NJ)],
@@ -517,22 +459,6 @@
         hidden_in, expert_ids.T, route_weight.T, gate_codes, up_codes, down_codes,
         gate_scales.transpose(0, 2, 1), up_scales.transpose(0, 2, 1), down_scales, bucket_owner,
     )
-    return pl.pallas_call(
-        mix_kernel,
-        out_shape=jax.ShapeDtypeStruct((TOK, D), bf16),
-        in_specs=[anys, anys],
-        out_specs=anys,
-        scratch_shapes=[
-            pltpu.VMEM((TOK, 256), bf16),
-            pltpu.VMEM((SLOTS, D), bf16),
-            pltpu.VMEM((TOK, D), bf16),
-            dma(()),
-            dma((TILES,)),
-            dma((TILES,)),
-        ],
-        compiler_params=pltpu.CompilerParams(vmem_limit_bytes=56 * 1024 * 1024),
-        name="mix",
-    )(comb, es)
 
 
 def solution(mesh):

time: 144 us -> 139 us (0.965)
  Pallas kernels: 144 us -> 137 us
  local copies, waits for them, and re-layouts: 0 us -> 1.84 us
    pallas_call x2 -> x1, Pallas kernels: 144 us -> 137 us  [on_device(): pl.pallas_call(kernel, out_shape=pltpu.VMEM((TOK, D), bf16), in_specs=[an...]
    unnamed x0 -> x1, local copies, waits for them, and re-layouts: none -> 1.84 us
where the time goes in v3:
time: 139 us
  Pallas kernels  137 us (99%)
  local copies, waits for them, and re-layouts  1.84 us (1%)
    pallas_call x1, Pallas kernels, on_device(): pl.pallas_call(kernel, out_shape=pltpu.VMEM((TOK, D), bf16), in_specs=[an...  137 us

profile of v3, /device:TPU:1, one launch (start us, length us, event | category | flops | bytes accessed | tf_op | source)
XLA Modules:
  0.0 139.0 jit_solution(16057497464784298923)
XLA Ops:
  0.0 137.1 %experts.1 = bf16[256,7168]{1,0:T(8,128)(2,1)S(1)} custom-call(bf16[256,7168]{1,0:T(8,128)(2,1)} %hid_hbm.1, s32[8,256]{1,0:T(8,128)} %bitcast.4, f32[8,256]{1,0:T(8,128)} %bitcast.5, bf16[1,896,256]{2,1,0:T(8,128)(2,1)} %gc_hbm.1, bf16[1,896,256]{2,1,0:T(8,128)(2,1)} %uc_hbm.1, bf16[1,256,896]{2,1,0:T(8,128)(2,1)} %dc_hbm.1, bf16[1,2,7]{2,1,0:T(2,128)(2,1)} %bitcast.6, ...), custom_call_target="tpu_custom_call" | custom-call | tf_op jit(solution)/shard_map/experts/pallas_call | solution.py:412
  137.1 1.8 %copy.12 = bf16[256,7168]{1,0:T(8,128)(2,1)} copy(bf16[256,7168]{1,0:T(8,128)(2,1)S(1)} %experts.1) | data formatting | bytes 7340032

commit v4 on v3

--- a/solution.py
+++ b/solution.py
@@ -19,7 +19,7 @@
 ROWS = PLANE * CAP
 SUB = 128
 NJ = BUCKET // SUB
-FROM = 3 * SLOTS
+FROM = 3 * LIVE
 MESH = pl.DeviceIdType.MESH
 
 SPREAD = (
@@ -28,13 +28,13 @@
 )
 
 PLAN = (
-    "c0 b0 U1 a0",
-    "b1 c1 a1 G1",
-    "a2 U2 B0-2 B2-4",
-    "B4-6 G2 B6-8 B8-10",
-    "U3 G3 b2 c2",
+    "a0 b0 G1 c0",
+    "U1 a1 b1 G2",
+    "c1 B0-2 U2 B2-4",
+    "a2 B4-6 B6-8 B8-10",
+    "G3 U3 b2 c2",
     "a3 d0 B10-12 B12-14",
-    "U4 G4 b3 e0",
+    "G4 U4 b3 e0",
     "B14-16 c3 a4 H",
     "d1 f0 Da b4",
     "e1 c4 Db d2",
@@ -186,7 +186,9 @@
             d_arrived(j, w, h)
             if h < 4:
                 d_ring(j, w, h).start()
-        for w in (0, 1):
+            else:
+                d_sib(j, w, h).start()
+        for w in (0, 1) if h < 4 else ():
             d_sib(j, w, h).start()
 
     loads[0].wait()
@@ -284,12 +286,9 @@
         acc[p, 1] += jnp.dot(xb, U[s], preferred_element_type=jnp.float32)
         return carry
 
-    def rows(xx, yy):
-        return rows16(xx * 4 + yy)
-
     def ret_copy(j, xx, yy, part):
         return copy(
-            Ps[j].at[:, rows(xx, yy), :], Rs[j].at[:, rows(part, y), :],
+            Ps[j].at[xx * 4 + yy], Rs[j].at[part * 4 + y],
             ret_s.at[j], ret_r.at[j], plane(xx, yy),
         )
 
@@ -305,42 +304,39 @@
             out = jnp.dot(H[:, :HID], near, preferred_element_type=jnp.float32) + jnp.dot(
                 H[:, HID:], far, preferred_element_type=jnp.float32
             )
-            Ps[j][b] = out[:, :SUB].astype(jnp.bfloat16)
-            Ps[j][b + 1] = out[:, SUB:].astype(jnp.bfloat16)
+            out = out.astype(jnp.bfloat16)
+            Ps[j][:, b] = out[:, :SUB].reshape(PLANE, CAP, SUB)
+            Ps[j][:, b + 1] = out[:, SUB:].reshape(PLANE, CAP, SUB)
         for w, xx in ((0, x_right), (1, x_left)):
-            some = pl.ds(pl.multiple_of(x_far * SLOTS + w * 32, 32), 32)
-            copy(
-                Ps[j].at[:, some, :], As[j].at[w], ret_s.at[j], ret_ra.at[j], plane(xx, y)
-            ).start()
+            some = Ps[j].at[pl.ds(x_far * 4 + w * 2, 2)]
+            copy(some, As[j].at[w], ret_s.at[j], ret_ra.at[j], plane(xx, y)).start()
         for k in (0, 1):
             ret_copy(j, x_right, 2 + k, 1).start()
             ret_copy(j, x_left, k, 2).start()
         for dy in (1, 3, 2):
             ret_copy(j, x, (y + dy) % 4, 0).start()
-        Rs[j][:, rows(0, y), :] = Ps[j][:, rows(x, y), :]
+        Rs[j][y] = Ps[j][x * 4 + y]
 
     def relay(j):
         copy(As[j], As[j], ret_s.at[j], ret_ra.at[j], sib_dev).wait_recv()
         for w, xx in ((0, x_right), (1, x_left)):
-            some = pl.ds(pl.multiple_of(xx * SLOTS + w * 32, 32), 32)
-            Ps[j][:, some, :] = (
-                Ps[j][:, some, :].astype(jnp.float32) + As[j][w].astype(jnp.float32)
+            some = pl.ds(xx * 4 + w * 2, 2)
+            Ps[j][some] = (
+                Ps[j][some].astype(jnp.float32) + As[j][w].astype(jnp.float32)
             ).astype(jnp.bfloat16)
         for k in (0, 1):
             ret_copy(j, x_right, k, 1).start()
             ret_copy(j, x_left, 2 + k, 2).start()
 
     def finish(j):
-        got = Rs[j].at[:, pl.ds(0, 11 * CAP), :]
-        copy(got, got, ret_s.at[j], ret_r.at[j], sib_dev).wait_recv()
+        some = Rs[j].at[pl.ds(0, 11)]
+        copy(some, some, ret_s.at[j], ret_r.at[j], sib_dev).wait_recv()
         sums = []
         for b in range(NB):
-            total = Rs[j][b, 0:SLOTS, :].astype(jnp.float32)
+            total = Rs[j][0:4, b].astype(jnp.float32)
             for part in (1, 2):
-                total = total + Rs[j][b, part * SLOTS : (part + 1) * SLOTS, :].astype(
-                    jnp.float32
-                )
-            sums.append(total.astype(jnp.bfloat16))
+                total = total + Rs[j][part * 4 : part * 4 + 4, b].astype(jnp.float32)
+            sums.append(total.astype(jnp.bfloat16).reshape(SLOTS, SUB))
         for b in range(0, NB, 2):
             pair = jnp.concatenate(sums[b : b + 2], axis=1)
             mixed = jnp.dot(
@@ -396,7 +392,7 @@
         some = Ds[j].at[pl.ds(0, 8)]
         copy(some, some, dsib_s.at[j], dsib_r.at[j], sib_dev).wait_send()
     for j in range(NJ):
-        some = Ps[j].at[:, pl.ds(0, 2 * 32 + 11 * CAP), :]
+        some = Ps[j].at[pl.ds(0, 15)]
         copy(some, some, ret_s.at[j], ret_r.at[j], sib_dev).wait_send()
 
 
@@ -424,9 +420,9 @@
             pltpu.VMEM((NB, TOK, BUCKET), bf16),
             pltpu.VMEM((2, 2, ROWS, HID), jnp.float32),
             pltpu.VMEM((ROWS, 2 * HID), bf16),
-            [pltpu.VMEM((NB, ROWS, SUB), bf16) for _ in range(NJ)],
-            [pltpu.VMEM((2, NB, 32, SUB), bf16) for _ in range(NJ)],
-            [pltpu.VMEM((NB, FROM, SUB), bf16) for _ in range(NJ)],
+            [pltpu.VMEM((PLANE, NB, CAP, SUB), bf16) for _ in range(NJ)],
+            [pltpu.VMEM((2, 2, NB, CAP, SUB), bf16) for _ in range(NJ)],
+            [pltpu.VMEM((FROM, NB, CAP, SUB), bf16) for _ in range(NJ)],
             pltpu.VMEM((8, 128), jnp.int32),
             pltpu.VMEM((8, 128), jnp.int32),
             pltpu.SMEM((8, 128), jnp.int32),

time: 139 us -> 139 us (level)
  no operation moved by 1% of the time
where the time goes in v4:
time: 139 us; the launch traced here: 138 us
  Pallas kernels  136 us (98%)
  local copies, waits for them, and re-layouts  1.84 us (1%)
    pallas_call x1, Pallas kernels, on_device(): pl.pallas_call(kernel, out_shape=pltpu.VMEM((TOK, D), bf16), in_specs=[an...  136 us

profile of v4, /device:TPU:1, one launch (start us, length us, event | category | flops | bytes accessed | tf_op | source)
XLA Modules:
  0.0 138.3 jit_solution(2798410268736127385)
XLA Ops:
  0.0 136.4 %experts.1 = bf16[256,7168]{1,0:T(8,128)(2,1)S(1)} custom-call(bf16[256,7168]{1,0:T(8,128)(2,1)} %hid_hbm.1, s32[8,256]{1,0:T(8,128)} %bitcast.4, f32[8,256]{1,0:T(8,128)} %bitcast.5, bf16[1,896,256]{2,1,0:T(8,128)(2,1)} %gc_hbm.1, bf16[1,896,256]{2,1,0:T(8,128)(2,1)} %uc_hbm.1, bf16[1,256,896]{2,1,0:T(8,128)(2,1)} %dc_hbm.1, bf16[1,2,7]{2,1,0:T(2,128)(2,1)} %bitcast.6, ...), custom_call_target="tpu_custom_call" | custom-call | tf_op jit(solution)/shard_map/experts/pallas_call | solution.py:408
  136.4 1.8 %copy.12 = bf16[256,7168]{1,0:T(8,128)(2,1)} copy(bf16[256,7168]{1,0:T(8,128)(2,1)S(1)} %experts.1) | data formatting | bytes 7340032
